TPU v7x, 256 devices: a whole 4x4x8 slice. The times are simulated.
256 devices in a mesh: row: 32 (over z, y), col: 8 (over x, core).
Axes of the slice: x: 4, y: 4, z: 8, core: 2. Of those that a mesh axis runs over, the one named last changes fastest.
Arguments:
- acts: bfloat16 [2048, 8192], P('col', 'row'), may hold values from -6 to 6
- output_cotangent: bfloat16 [2048, 28672], P('row', 'col'), may hold values from -0.29882812 to 0.29882812
- frozen: bfloat16 [8192, 28672], P('row', 'col'), may hold values from -0.0625 to 0.0625
- down_factors: float32 [4, 16, 28672], P(None, None, 'col'), may hold values from -0.10630251 to 0.10630251
- up_factors: float32 [4, 8192, 16], P(None, 'row'), may hold values from -0.19887379 to 0.19887379
- magnitude: float32 [4, 28672], P(None, 'col'), may hold values from 0.5 to 2
- slot_trial_index: int32 [16], replicated, may hold values from 0 to 3, as said below
Outputs:
- activation_gradient: bfloat16 [2048, 8192], P('col', 'row')
- magnitude_gradient: float32 [4, 28672], P(None, 'col')
- down_factor_gradient: float32 [4, 16, 28672], P(None, None, 'col')
- up_factor_gradient: float32 [4, 8192, 16], P(None, 'row')
Inputs may be any that keep to these rules, and one draw needn't show every extreme that they name: `slot_trial_index`: each of the 4 trials is named by exactly 4 slots.
All inputs are finite; a program needn't handle non-finite values.
Results may differ from a plain program's by a relative error of at most 0.0049.
Values may be sent and summed in bfloat16 or wider, within the bound.
A program may use at most 192 MiB of HBM per device.

v0:
```python
import jax
import jax.numpy as jnp
from jax import lax
from jax.sharding import PartitionSpec as P

ADAPTER_SCALE = 2.0
EPS = 1e-06
HIGH_PRECISION = lax.Precision.HIGHEST
FAST = lax.Precision.HIGH


def local(acts, output_cotangent, frozen, down_factors, up_factors, magnitude, slot_trial_index):
    trial_range, rank_index, block_columns = down_factors.shape
    block_width = frozen.shape[0]
    xall = lax.all_gather(acts, "col", axis=0, tiled=True)
    total = xall.shape[0]
    slot_len = total // slot_trial_index.shape[0]
    owner_ids = jnp.repeat(slot_trial_index, slot_len, total_repeat_length=total)
    owner = (owner_ids[:, None] == jnp.arange(trial_range, dtype=jnp.int32)[None, :]).astype(
        jnp.float32
    )
    spread = jnp.repeat(owner, rank_index, axis=1)
    stacked_up_factors = jnp.transpose(up_factors, (1, 0, 2)).reshape(
        block_width, trial_range * rank_index
    )
    stacked_down_factors = down_factors.reshape(trial_range * rank_index, block_columns)
    xfull = xall.astype(jnp.float32)
    qmat = jnp.dot(xfull, stacked_up_factors, precision=HIGH_PRECISION) * spread
    full_weight = frozen.astype(jnp.float32)
    k0_part = jnp.dot(stacked_up_factors.T, full_weight, precision=HIGH_PRECISION)
    gram_piece = jnp.einsum("mwz,mwe->mze", up_factors, up_factors, precision=HIGH_PRECISION)
    first = jnp.stack(
        [
            jnp.sum(
                jnp.square(
                    full_weight
                    + ADAPTER_SCALE
                    * jnp.dot(
                        up_factors[trial_index], down_factors[trial_index], precision=HIGH_PRECISION
                    )
                ),
                axis=0,
            )
            for trial_index in range(trial_range)
        ]
    )
    first_sum, k0_sum, gram_total = lax.psum((first, k0_part, gram_piece), "row")
    k0_trial = k0_sum.reshape(trial_range, rank_index, block_columns)
    down_factor_gram = jnp.einsum(
        "oya,oar->oyr", gram_total, down_factors, precision=HIGH_PRECISION
    )
    col_norm = jnp.sqrt(first_sum + EPS)
    col_norm, rescale_factor, key_matrix_term = (
        col_norm,
        magnitude / col_norm,
        k0_trial + ADAPTER_SCALE * down_factor_gram,
    )
    piece = lax.all_gather(output_cotangent, "row", axis=0, tiled=True)
    block_start = jnp.int32(0)
    dx_acc = jnp.zeros((total, block_width), jnp.float32)
    dc_acc = jnp.zeros((trial_range, block_columns), jnp.float32)
    qdy_acc = jnp.zeros((trial_range * rank_index, block_columns), jnp.float32)
    xp_acc = jnp.zeros((block_width, trial_range * rank_index), jnp.float32)
    rows = piece.shape[0]
    qrows = lax.dynamic_slice_in_dim(qmat, block_start, rows, 0)
    hrows = lax.dynamic_slice_in_dim(owner, block_start, rows, 0)
    srows = lax.dynamic_slice_in_dim(spread, block_start, rows, 0)
    pre = jnp.dot(xall, frozen, preferred_element_type=jnp.float32) + ADAPTER_SCALE * jnp.dot(
        qrows, stacked_down_factors, precision=FAST
    )
    dyf = piece.astype(jnp.float32)
    dc_term = jnp.dot(hrows.T, dyf * pre, precision=FAST)
    qdy_term = jnp.dot(qrows.T, dyf, precision=FAST)
    dzb = (piece.astype(jnp.float32) * jnp.dot(hrows, rescale_factor, precision=FAST)).astype(
        jnp.bfloat16
    )
    prows = jnp.dot(dzb.astype(jnp.float32), stacked_down_factors.T, precision=FAST) * srows
    dzb, prows = (dzb, prows)
    dxrows = jnp.dot(dzb, frozen.T, preferred_element_type=jnp.float32) + ADAPTER_SCALE * jnp.dot(
        prows, stacked_up_factors.T, precision=HIGH_PRECISION
    )
    dx_acc = lax.dynamic_update_slice_in_dim(dx_acc, dxrows, block_start, 0)
    xp_acc = xp_acc + jnp.dot(xfull.T, prows, precision=HIGH_PRECISION)
    dc_part = dc_acc + dc_term
    qdy_part = qdy_acc + qdy_term
    dscale, qdy_sum = lax.psum((dc_part, qdy_part), "row")
    activation_gradient = lax.psum_scatter(dx_acc, "col", scatter_dimension=0, tiled=True).astype(
        jnp.bfloat16
    )
    magnitude_gradient = dscale / col_norm
    gradient_factor = -dscale * magnitude / (col_norm * col_norm * col_norm)
    down_factor_gradient = ADAPTER_SCALE * (
        qdy_sum.reshape(trial_range, rank_index, block_columns) * rescale_factor[:, None, :]
        + key_matrix_term * gradient_factor[:, None, :]
    )
    scaled_down_factor = down_factors * gradient_factor[:, None, :]
    weight_gradient_step = jnp.dot(
        full_weight,
        scaled_down_factor.reshape(trial_range * rank_index, block_columns).T,
        precision=HIGH_PRECISION,
    )
    inner_product = jnp.einsum(
        "bzg,big->bzi", scaled_down_factor, down_factors, precision=HIGH_PRECISION
    )
    up_factor_magnitude = jnp.einsum(
        "qmo,qor->qmr", up_factors, inner_product, precision=HIGH_PRECISION
    )
    up_factor_grad_piece = ADAPTER_SCALE * (
        jnp.transpose(
            (xp_acc + weight_gradient_step).reshape(block_width, trial_range, rank_index), (1, 0, 2)
        )
        + ADAPTER_SCALE * up_factor_magnitude
    )
    up_factor_gradient = lax.psum(up_factor_grad_piece, "col")
    return (activation_gradient, magnitude_gradient, down_factor_gradient, up_factor_gradient)


def solution(mesh):
    in_specs = (
        P("col", "row"),
        P("row", "col"),
        P("row", "col"),
        P(None, None, "col"),
        P(None, "row", None),
        P(None, "col"),
        P(),
    )
    out_specs = (P("col", "row"), P(None, "col"), P(None, None, "col"), P(None, "row", None))
    return jax.shard_map(local, mesh=mesh, in_specs=in_specs, out_specs=out_specs, check_vma=False)
```

profile of v0, /device:TPU:8, one launch (start us, length us, event | category | flops | bytes accessed | tf_op | source)
XLA Modules:
  0.0 601.2 jit_solution(10417932290582004760)
XLA Ops:
  8.7 5.2 fusion.17
  14.0 3.5 fusion.16
  17.5 3.5 fusion.15
  21.1 4.0 fusion.14
  25.2 0.7 fusion.47
  25.9 4.4 compare_select_fusion.1
  30.5 5.7 select_select_fusion
  36.2 0.8 fusion.53
  37.0 2.0 fusion.52
  39.7 0.8 copy-done.2
  40.5 2.3 convolution_multiply_fusion.6
  42.8 13.3 %fusion.49 = f32[2048,3584]{1,0:T(8,128)} fusion(bf16[2048,256]{1,0:T(8,128)(2,1)} %all-gather.5.cloned.1.call-done, bf16[256,3584]{1,0:T(8,128)(2,1)S(1)} %copy-done.1), kind=kOutput, calls=%fused_computation.89 | convolution fusion | flops 3758096384 | bytes 32243712 | tf_op jit(solution)/shard_map/dot_general | solution.py:68
  56.1 15.4 %fusion.50 = f32[2048,3584]{1,0:T(8,128)} fusion(f32[2048,64]{0,1:T(8,128)S(1)} %convolution_multiply_fusion.6, f32[64,3584]{1,0:T(8,128)S(1)} %bitcast.98), kind=kOutput, calls=%fused_computation.90 | convolution fusion | flops 2818572288 | bytes 30801920 | tf_op jit(solution)/shard_map/dot_general | solution.py:68
  71.5 98.6 %all-gather.3.cloned.1.call-done = bf16[2048,3584]{1,0:T(8,128)(2,1)} async-done(((bf16[64,3584]{1,0:T(8,128)(2,1)}), bf16[2048,3584]{1,0:T(8,128)(2,1)}) %all-gather.3.cloned.1.call-update) | async-done | bytes 14680080 | tf_op jit(solution)/shard_map/all_gather | solution.py:58
  170.0 25.0 %fusion.1 = f32[4,3584]{1,0:T(4,128)} fusion(bf16[2048,3584]{1,0:T(8,128)(2,1)} %all-gather.3.cloned.1.call-done, f32[2048,3584]{1,0:T(8,128)} %fusion.49, f32[2048,3584]{1,0:T(8,128)} %fusion.50, s32[2048]{0:T(1024)S(1)} %select_select_fusion), kind=kOutput, calls=%fused_computation.3 | convolution fusion | flops 205529088 | bytes 73465856 | tf_op jit(solution)/shard_map/dot_general | solution.py:72
  195.2 9.3 %fusion.51 = f32[64,3584]{1,0:T(8,128)} fusion(f32[2048,64]{0,1:T(8,128)S(1)} %convolution_multiply_fusion.6, bf16[2048,3584]{1,0:T(8,128)(2,1)} %all-gather.3.cloned.1.call-done), kind=kOutput, calls=%fused_computation.91 | convolution fusion | flops 2818572288 | bytes 16121856 | tf_op jit(solution)/shard_map/dot_general | solution.py:73
  204.7 131.0 %all-reduce.8.cloned.1.call-done = (f32[4,3584]{1,0:T(4,128)}, f32[4,3584]{1,0:T(4,128)}, f32[4,16,16]{2,1,0:T(8,128)}) async-done(((f32[4,3584]{1,0:T(4,128)}, f32[4,3584]{1,0:T(4,128)}, f32[4,16,16]{2,1,0:T(8,128)}), (f32[4,3584]{1,0:T(4,128)}, f32[4,3584]{1,0:T(4,128)}, f32[4,16,16]{2,1,0:T(8,128)})) %all-reduce.8.cloned.1.call-update) | async-done | bytes 118800 | tf_op jit(solution)/shard_map/psum | solution.py:47
  335.7 1.5 fusion.30
  337.3 15.1 %fusion = bf16[2048,3584]{1,0:T(8,128)(2,1)} fusion(bf16[2048,3584]{1,0:T(8,128)(2,1)} %all-gather.3.cloned.1.call-done, f32[4,3584]{1,0:T(4,128)S(1)} %get-tuple-element.34, s32[2048]{0:T(1024)S(1)} %select_select_fusion), kind=kOutput, calls=%fused_computation.2 | convolution fusion | flops 198189056 | bytes 29425664 | tf_op jit(solution)/shard_map/dot_general | solution.py:74
  352.4 12.2 %convolution_multiply_fusion.7 = f32[2048,64]{0,1:T(8,128)S(1)} fusion(f32[2048,64]{0,1:T(8,128)S(1)} %bitcast.101, bf16[2048,3584]{1,0:T(8,128)(2,1)} %fusion, f32[64,3584]{1,0:T(8,128)S(1)} %bitcast.99), kind=kOutput, calls=%fused_computation.27 | convolution fusion | flops 2818703360 | bytes 16646144 | tf_op jit(solution)/shard_map/dot_general | solution.py:77
  364.6 7.3 %fusion.48 = f32[2048,256]{1,0:T(8,128)S(1)} fusion(bf16[2048,3584]{1,0:T(8,128)(2,1)} %fusion, bf16[256,3584]{1,0:T(8,128)(2,1)S(1)} %copy-done.1), kind=kOutput, calls=%fused_computation.88 | convolution fusion | flops 3758096384 | bytes 18612224 | tf_op jit(solution)/shard_map/dot_general | solution.py:79
  371.9 3.3 fusion.13
  375.5 1.9 fusion.54
  377.4 1.3 fusion.21
  378.7 1.8 convolution_add_fusion
  380.5 0.8 fusion.20
  381.4 108.3 %all-reduce.10.cloned.1.call-done = (f32[4,16,3584]{2,1,0:T(8,128)}, f32[4,16,3584]{2,1,0:T(8,128)}) async-done(((f32[4,16,3584]{2,1,0:T(8,128)}, f32[4,16,3584]{2,1,0:T(8,128)}), (f32[4,16,3584]{2,1,0:T(8,128)}, f32[4,16,3584]{2,1,0:T(8,128)})) %all-reduce.10.cloned.1.call-update) | async-done | bytes 1835024 | tf_op jit(solution)/shard_map/psum | solution.py:47
  489.7 3.4 fusion.12
  493.2 34.0 %reduce-scatter.2.cloned.1.call-done = f32[256,256]{1,0:T(8,128)} async-done(((f32[2048,256]{1,0:T(8,128)}), f32[256,256]{1,0:T(8,128)}) %reduce-scatter.2.cloned.1.call-update) | async-done | bytes 262160 | tf_op jit(solution)/shard_map/reduce_scatter | solution.py:87
  527.2 1.6 convert_element_type.22
  528.8 63.9 %all-reduce.6.cloned.1.call-done = f32[4,256,16]{1,2,0:T(8,128)} async-done(((f32[4,256,16]{1,2,0:T(8,128)}), f32[4,256,16]{1,2,0:T(8,128)}) %all-reduce.6.cloned.1.call-update) | async-done | bytes 65552 | tf_op jit(solution)/shard_map/psum | solution.py:114
  592.7 1.5 copy.17
  (39 shorter events, 3.2 us)
Async XLA Ops:
  7.2 6.8 %copy-start.4 = (f32[4,256,16]{1,2,0:T(8,128)S(1)}, f32[4,256,16]{1,2,0:T(8,128)}, u32[]{:S(2)}) copy-start(f32[4,256,16]{1,2,0:T(8,128)} %param.13) | copy-start | bytes 196612
  7.2 6.8 %copy-start = (f32[4,16,3584]{2,1,0:T(8,128)S(1)}, f32[4,16,3584]{2,1,0:T(8,128)}, u32[]{:S(2)}) copy-start(f32[4,16,3584]{2,1,0:T(8,128)} %param.12) | copy-start | bytes 2752516
  7.2 6.8 %copy-start.1 = (bf16[256,3584]{1,0:T(8,128)(2,1)S(1)}, bf16[256,3584]{1,0:T(8,128)(2,1)}, u32[]{:S(2)}) copy-start(bf16[256,3584]{1,0:T(8,128)(2,1)} %param.11) | copy-start | bytes 5505028
  7.2 32.5 %all-gather.5.cloned.1.call-start = ((), (), s32[]{:S(2)}) async-start(), calls=%async_computation.3 | async-start | bytes 1179648 | tf_op jit(solution)/shard_map/all_gather | solution.py:15
  7.9 162.1 %all-gather.3.cloned.1.call-start = ((), (), s32[]{:S(2)}) async-start(), calls=%async_computation.1 | async-start | bytes 15138816 | tf_op jit(solution)/shard_map/all_gather | solution.py:58
  8.7 327.1 %all-reduce.8.cloned.1.call-start = ((), (), s32[]{:S(2)}) async-start(), calls=%async_computation.5 | async-start | bytes 294912 | tf_op jit(solution)/shard_map/psum | solution.py:47
  17.5 7.6 %copy-start.5 = (s32[16]{0:T(128)S(1)}, s32[16]{0:T(128)}, u32[]{:S(2)}) copy-start(s32[16]{0:T(128)} %param.15) | copy-start | bytes 196
  39.7 0.8 copy-start.2
  195.1 140.6 %copy-start.6 = (f32[4,3584]{1,0:T(4,128)S(1)}, f32[4,3584]{1,0:T(4,128)}, u32[]{:S(2)}) copy-start(f32[4,3584]{1,0:T(4,128)} %param.14) | copy-start | bytes 172036
  195.1 294.6 %all-reduce.10.cloned.1.call-start = ((), (), s32[]{:S(2)}) async-start(), calls=%async_computation.6 | async-start | bytes 3670016 | tf_op jit(solution)/shard_map/psum | solution.py:47
  204.5 322.7 %reduce-scatter.2.cloned.1.call-start = ((), (), s32[]{:S(2)}) async-start(), calls=%async_computation.2 | async-start | bytes 2359296 | tf_op jit(solution)/shard_map/reduce_scatter | solution.py:87
  337.3 15.1 %copy-start.3 = (f32[2048,4,16]{0,2,1:T(8,128)S(1)}, f32[2048,4,16]{0,2,1:T(8,128)}, u32[]{:S(2)}) copy-start(f32[2048,4,16]{0,2,1:T(8,128)} %copy-done.2) | copy-start | bytes 1572868
  375.2 217.4 %all-reduce.6.cloned.1.call-start = ((), (), s32[]{:S(2)}) async-start(), calls=%async_computation.4 | async-start | bytes 131072 | tf_op jit(solution)/shard_map/psum | solution.py:114
  377.4 112.4 %copy-start.7 = (f32[4,16,16]{2,1,0:T(8,128)S(1)}, f32[4,16,16]{2,1,0:T(8,128)}, u32[]{:S(2)}) copy-start(f32[4,16,16]{2,1,0:T(8,128)} %get-tuple-element.27) | copy-start | bytes 12292
Sparse Core Ops, SparseCore 0:
  9.9 28.7 all-gather.4
  41.3 128.7 all-gather.2
  195.2 140.4 all-reduce.7
  340.2 149.4 all-reduce.9
  492.3 34.8 reduce-scatter.1
  530.0 62.6 all-reduce.5
where the time goes:
time: 610 us; the launch traced here: 601 us
  waiting for transfers between devices  437 us (72%)
  matrix products  131 us (21%)
  between operations  14.6 us (2%)
  other arithmetic  14.3 us (2%)
    psum x2, waiting for transfers between devices, local(): lax.psum((first, k0_part, gram_piece), 'row')  239 us
    all_gather x1, waiting for transfers between devices, local(): piece = lax.all_gather(output_cotangent, 'row', axis=0, tiled=True)  98.6 us
    psum x1, waiting for transfers between devices, local(): up_factor_gradient = lax.psum(up_factor_grad_piece, 'col')  63.9 us
    reduce_scatter x1, waiting for transfers between devices, local(): lax.psum_scatter(dx_acc, 'col', scatter_dimension=0, tiled=True)  34 us
    dot_general x1, matrix products, local(): dc_term = jnp.dot(hrows.T, dyf * pre, precision=FAST)  25 us
    dot_general x4, matrix products, local(): jnp.dot(up_factors[trial_index], down_factors[trial_index], precision=HIG...  16.3 us
    dot_general x1, matrix products, local(): jnp.dot(qrows, stacked_down_factors, precision=FAST)  15.4 us
    dot_general x1, matrix products, local(): jnp.dot(hrows, rescale_factor, precision=FAST)  15.1 us
  transfers between devices with their start and end apart: 6, of which 5 were waited for; matrix products, arithmetic and copies ran while one was open for 20% of the time, Pallas kernels for 0%

commit v1 on v0

v1 whole, which is shorter than its diff:
```python
import functools

import jax
import jax.numpy as jnp
from jax import lax
from jax.experimental import pallas as pl
from jax.experimental.pallas import tpu as pltpu
from jax.sharding import PartitionSpec as P

SCALE = 2.0
EPS = 1e-06
NX, NY, NZ = 4, 4, 8
MESH = pl.DeviceIdType.MESH
F32, BF16 = jnp.float32, jnp.bfloat16
RP = 128


def mm(a, b, ca, cb, precision=None):
    return lax.dot_general(
        a, b, (((ca,), (cb,)), ((), ())), precision=precision, preferred_element_type=F32
    )


def kernel(
    acts, dy, w, dn, ut, mag, idx,
    out_dx, out_mag, out_dn, out_up,
    dyA, X, Wg, Wo, Ug, Uo, UTs, Df, Dq, Db,
    nyS, nyR, nzS, nzR, resS,
    dsS, dsR, gfS, qacc, kacc, xpT, qkS, qkR,
    dxo, dxs, pairR, xs, xR, ysS, ysR,
    upS, upR, upP, upPR, upX, upXR, mgR, dnQ,
    ss, rs, ls, ps, pr, xss, xrs,
):
    row, col = lax.axis_index("row"), lax.axis_index("col")
    z, y = lax.div(row, NY), lax.rem(row, NY)
    x, k = lax.div(col, 2), lax.rem(col, 2)
    rank = 16
    trials = 4
    rows = dy.shape[0]
    cols = w.shape[1]
    qc = cols // NY
    wd = w.shape[0]
    tok = acts.shape[0]

    def mod(v, n):
        return lax.rem(v + n, n)

    def at_y(j):
        return (z * NY + mod(y + j, NY), col)

    def at_z(j):
        return (mod(z + j, NZ) * NY + y, col)

    def at_x(j):
        return (row, mod(x + j, NX) * 2 + k)

    sib = (row, x * 2 + 1 - k)
    YJ, XJ = (1, 3, 2), (1, 3, 2)

    barrier = pltpu.get_barrier_semaphore()
    peers = [at_y(j) for j in YJ] + [at_x(j) for j in XJ] + [at_z(j) for j in range(1, NZ)] + [sib]
    for p in peers:
        pl.semaphore_signal(barrier, inc=1, device_id=p, device_id_type=MESH)
    pl.semaphore_wait(barrier, len(peers))

    count = [0, 0]
    sent = []

    def remote(src, dst, dev, start=True):
        i = count[0]
        count[0] += 1
        d = pltpu.make_async_remote_copy(
            src_ref=src, dst_ref=dst, send_sem=ss.at[i], recv_sem=rs.at[i],
            device_id=dev, device_id_type=MESH,
        )
        if start:
            d.start()
        sent.append(d)
        return d

    def localcp(src, dst):
        i = count[1]
        count[1] += 1
        d = pltpu.make_async_copy(src, dst, ls.at[i])
        d.start()
        return d

    def yq(j):
        return pl.ds(pl.multiple_of(mod(y + j, NY) * qc, 128), qc)

    yrows = pl.ds(pl.multiple_of(y * rows, rows), rows)
    ywd = pl.ds(pl.multiple_of(y * wd, wd), wd)

    dy_local = localcp(dy.at[:, yq(0)], dyA.at[z, yrows, :])
    dy_y = [remote(dy.at[:, yq(j)], dyA.at[z, yrows, :], at_y(j)) for j in YJ]
    ut_local = localcp(ut, UTs.at[pl.ds(0, trials * rank), :])
    act_local = localcp(acts, X.at[col, :, ywd])
    act_y = [remote(acts, X.at[col, :, ywd], at_y(j)) for j in YJ]
    df_local = localcp(dn, Df.at[pl.ds(0, trials * rank), :])
    wo_local = localcp(w, Wo)
    UTs[trials * rank :, :] = jnp.zeros((RP - trials * rank, wd), F32)
    Df[trials * rank :, :] = jnp.zeros((RP - trials * rank, cols), F32)
    ut_local.wait()
    Uo[...] = UTs[...].T.astype(BF16)
    u_local = localcp(Uo, Ug.at[ywd, :])
    u_y = [remote(Uo, Ug.at[ywd, :], at_y(j)) for j in YJ]
    wg_local = localcp(w.at[:, yq(0)], Wg.at[ywd, :])
    w_y = [remote(w.at[:, yq(j)], Wg.at[ywd, :], at_y(j)) for j in YJ]

    ring = {}

    def zsend(sign, step, b):
        ys = mod(y - (0, 1, 3, 2)[b], NY)
        src = dyA.at[
            mod(z - sign * (step - 1), NZ), pl.ds(pl.multiple_of(ys * rows, rows), rows), :
        ]
        ring[sign, step, b] = remote(src, src, at_z(sign))

    def zstep(step, b):
        for sign in (1, -1):
            if step > 1:
                ring[sign, step - 1, b].wait_recv()
            if step < 4 or (b < 2) == (sign == 1):
                zsend(sign, step, b)

    dy_local.wait()
    zstep(1, 0)
    for b, d in enumerate(dy_y):
        d.wait_recv()
        zstep(1, b + 1)

    df_local.wait()
    wo_local.wait()
    nyS[...] = jnp.zeros_like(nyS)
    half = qc // 2

    def norm_piece(yy):
        for h in range(2):
            c0 = yy * qc + h * half
            wb = Wo[:, c0 : c0 + half].astype(F32)
            db = (SCALE * Df[:, c0 : c0 + half]).astype(BF16)
            owner = lax.broadcasted_iota(jnp.int32, db.shape, 0) // rank
            for t in range(trials):
                m = wb + mm(Uo[...], jnp.where(owner == t, db, jnp.zeros_like(db)), 1, 0)
                nyS[yy, t : t + 1, h * half : (h + 1) * half] = jnp.sum(m * m, axis=0, keepdims=True)

    for yy in range(NY):
        norm_piece(yy)
        zstep(2, yy)
    ny_y = [remote(nyS.at[mod(y + j, NY)], nyR.at[y], at_y(j)) for j in YJ]
    zstep(3, 0)
    act_local.wait()
    for d in act_y:
        d.wait_recv()
    x_x = [remote(X.at[col], X.at[col], at_x(j)) for j in XJ]
    x_sib = [remote(X.at[col], X.at[col], sib)]
    zstep(3, 1)
    for d in ny_y:
        d.wait_recv()
    nzS[...] = (
        nyS[y] + nyR[mod(y + 1, NY)] + nyR[mod(y + 2, NY)] + nyR[mod(y + 3, NY)]
    )
    nz_z = [remote(nzS, nzR.at[z], at_z(j)) for j in range(1, NZ)]
    zstep(3, 2)
    zstep(3, 3)
    dq_load = Df[:, pl.ds(pl.multiple_of(y * qc, 128), qc)]
    Dq[...] = dq_load
    Db[...] = dq_load.astype(BF16)
    for b in range(NY):
        zstep(4, b)
    for j, d in zip(XJ, x_x):
        d.wait_recv()
        src = X.at[mod(x - j, NX) * 2 + k]
        x_sib.append(remote(src, src, sib))
    u_local.wait()
    wg_local.wait()
    for d in u_y + w_y:
        d.wait_recv()

    same = (
        lax.broadcasted_iota(jnp.int32, (RP, RP), 0) // rank
        == lax.broadcasted_iota(jnp.int32, (RP, RP), 1) // rank
    )
    gram = jnp.where(same, mm(Ug[...], Ug[...], 0, 0), 0.0)
    kacc[...] = mm(Ug[...], Wg[...], 0, 0) + SCALE * mm(gram.astype(BF16), Db[...], 1, 0)

    for d in nz_z:
        d.wait_recv()
    nsq = nzS[...]
    for j in range(1, NZ):
        nsq = nsq + nzR[mod(z + j, NZ)]
    norm = jnp.sqrt(nsq[:trials] + EPS)
    magq = mag[:, pl.ds(pl.multiple_of(y * qc, 128), qc)]
    resS[0:trials, :] = magq / norm

    for d in x_sib:
        d.wait_recv()
    for key in ((1, 4, 0), (1, 4, 1), (-1, 4, 2), (-1, 4, 3)):
        ring[key].wait_recv()

    dsS[...] = jnp.zeros_like(dsS)
    qacc[...] = jnp.zeros_like(qacc)
    xpT[...] = jnp.zeros_like(xpT)
    hrow = tok // 2

    def chunk_of(i):
        s = lax.div(i + 1, 2)
        return lax.rem(z + s * (2 * lax.rem(i, 2) - 1) + NZ, NZ)

    def pair_copy(slot):
        return pltpu.make_async_remote_copy(
            src_ref=dxs.at[slot], dst_ref=pairR.at[slot], send_sem=ps.at[slot],
            recv_sem=pr.at[slot], device_id=sib, device_id_type=MESH,
        )

    def x_copy(to, frm):
        return pltpu.make_async_remote_copy(
            src_ref=xs.at[to], dst_ref=xR.at[frm], send_sem=xss.at[to],
            recv_sem=xrs.at[frm], device_id=(row, to * 2 + k), device_id_type=MESH,
        )

    def compute(i):
        c = chunk_of(i)
        xc = X[c]
        dyc = dyA[c]
        t0, t1 = idx[2 * c], idx[2 * c + 1]
        sub = lax.broadcasted_iota(jnp.int32, (tok, RP), 0)
        lane = lax.broadcasted_iota(jnp.int32, (tok, RP), 1)
        mask = lane // rank == jnp.where(sub < hrow, t0, t1)
        q = jnp.where(mask, mm(xc, Ug[...], 1, 0), 0.0).astype(BF16)
        pre = mm(xc, Wg[...], 1, 0) + SCALE * mm(q, Db[...], 1, 0)
        dyf = dyc.astype(F32)
        e = dyf * pre
        trow = lax.broadcasted_iota(jnp.int32, (8, qc), 0)
        s0 = jnp.sum(e[:hrow], axis=0, keepdims=True)
        s1 = jnp.sum(e[hrow:], axis=0, keepdims=True)
        dsS[...] += jnp.where(trow == t0, s0, 0.0) + jnp.where(trow == t1, s1, 0.0)
        res = resS[0:trials, :]
        r0 = jnp.zeros((1, qc), F32)
        r1 = jnp.zeros((1, qc), F32)
        for t in range(trials):
            r0 = jnp.where(t0 == t, res[t : t + 1], r0)
            r1 = jnp.where(t1 == t, res[t : t + 1], r1)
        gp = jnp.concatenate(
            [(dyf[:hrow] * r0).astype(BF16), (dyf[hrow:] * r1).astype(BF16)], axis=0
        )
        p = jnp.where(mask, mm(gp, Db[...], 1, 1), 0.0).astype(BF16)
        qacc[...] += mm(q, dyc, 0, 0)
        xpT[...] += mm(p, xc, 0, 0)
        dx = mm(gp, Wg[...], 1, 1) + SCALE * mm(p, Ug[...], 1, 1)
        slot = lax.div(c, 2)

        @pl.when(lax.rem(c, 2) == k)
        def _():
            dxo[slot] = dx

        @pl.when(lax.rem(c, 2) != k)
        def _():
            dxs[slot] = dx.astype(BF16)
            pair_copy(slot).start()

    def pass_on(i):
        c = chunk_of(i)
        slot = lax.div(c, 2)

        @pl.when(lax.rem(c, 2) == k)
        def _():
            pair_copy(slot).wait_recv()
            total = dxo[slot] + pairR[slot].astype(F32)

            @pl.when(slot == x)
            def _():
                dxo[slot] = total

            @pl.when(slot != x)
            def _():
                xs[slot] = total.astype(BF16)
                x_copy(slot, x).start()

    def step(i, carry):
        compute(i)

        @pl.when(i > 0)
        def _():
            pass_on(i - 1)

        return carry

    lax.fori_loop(0, NZ, step, 0)

    ds_z = [remote(dsS, dsR.at[z], at_z(j)) for j in range(1, NZ)]
    for zz in range(NZ):
        qkS[zz, 0:8, :] = qacc[8 * zz : 8 * zz + 8, :]
        qkS[zz, 8:16, :] = kacc[8 * zz : 8 * zz + 8, :]
    qk_z = [remote(qkS.at[mod(z + j, NZ)], qkR.at[z], at_z(j)) for j in range(1, NZ)]
    pass_on(NZ - 1)
    for d in ds_z:
        d.wait_recv()
    dsum = dsS[...]
    for j in range(1, NZ):
        dsum = dsum + dsR[mod(z + j, NZ)]
    dsum = dsum[:trials]
    mgR[y, 0:trials, :] = dsum / norm
    mg_y = [remote(mgR.at[y], mgR.at[y], at_y(j)) for j in YJ]
    gf = -dsum * magq / (norm * norm * norm)
    gfS[0:trials, :] = gf
    dg = jnp.concatenate(
        [Dq[rank * t : rank * (t + 1), :] * gf[t : t + 1] for t in range(trials)]
        + [jnp.zeros((RP - trials * rank, qc), F32)],
        axis=0,
    ).astype(BF16)
    inner = jnp.where(same, mm(dg, Db[...], 1, 1), 0.0).astype(BF16)
    up = SCALE * (xpT[...] + mm(dg, Wg[...], 1, 1) + SCALE * mm(inner, Ug[...], 1, 1))
    for yy in range(NY):
        upS[yy] = up[: trials * rank, yy * wd : (yy + 1) * wd]
    up_y = [remote(upS.at[mod(y + j, NY)], upR.at[y], at_y(j)) for j in YJ]

    for d in qk_z:
        d.wait_recv()
    qk = qkS[z]
    for j in range(1, NZ):
        qk = qk + qkR[mod(z + j, NZ)]
    tz = lax.div(z * 8, rank)
    zrows = pl.ds(pl.multiple_of(z * 8, 8), 8)
    dnQ[zrows, :] = SCALE * (
        qk[0:8] * resS[pl.ds(tz, 1), :] + qk[8:16] * gfS[pl.ds(tz, 1), :]
    )
    dn_z = [remote(dnQ.at[zrows, :], dnQ.at[zrows, :], at_z(j)) for j in range(1, NZ)]

    for d in up_y:
        d.wait_recv()
    upP[...] = upS[y] + upR[mod(y + 1, NY)] + upR[mod(y + 2, NY)] + upR[mod(y + 3, NY)]
    up_p = remote(upP, upPR, sib)

    for d in dn_z:
        d.wait_recv()
    dn_local = localcp(dnQ, out_dn.at[:, yq(0)])
    dn_y = [remote(dnQ, out_dn.at[:, yq(0)], at_y(j)) for j in YJ]

    up_p.wait_recv()
    upX[...] = upP[...] + upPR[...]
    up_x = [remote(upX, upXR.at[x], at_x(j)) for j in XJ]

    for j in (1, 2, 3):
        x_copy(mod(x + j, NX), mod(x + j, NX)).wait_recv()
    total = dxo[x]
    for j in (1, 2, 3):
        total = total + xR[mod(x + j, NX)].astype(F32)
    dxo[x] = total
    for yy in range(NY):
        ysS[yy] = total[:, yy * wd : (yy + 1) * wd].astype(BF16)
    ys_y = [remote(ysS.at[mod(y + j, NY)], ysR.at[y], at_y(j)) for j in YJ]

    for d in up_x:
        d.wait_recv()
    out_up[...] = upX[...] + upXR[mod(x + 1, NX)] + upXR[mod(x + 2, NX)] + upXR[mod(x + 3, NX)]
    for d in mg_y:
        d.wait_recv()
    for yy in range(NY):
        out_mag[:, yy * qc : (yy + 1) * qc] = mgR[yy, 0:trials, :]
    for d in ys_y:
        d.wait_recv()
    acc = dxo[x, :, pl.ds(pl.multiple_of(y * wd, wd), wd)]
    for j in (1, 2, 3):
        acc = acc + ysR[mod(y + j, NY)].astype(F32)
    out_dx[...] = acc.astype(BF16)

    for d in dn_y:
        d.wait_recv()
    dn_local.wait()
    for d in sent:
        d.wait_send()
    for slot in range(4):
        pair_copy(slot).wait_send()
    for j in (1, 2, 3):
        x_copy(mod(x + j, NX), x).wait_send()


def local(acts, dy, w, down, up, mag, idx):
    trials, rank, cols = down.shape
    wd = w.shape[0]
    tok = acts.shape[0]
    qc = cols // NY
    tr = trials * rank
    dn = down.reshape(tr, cols)
    ut = jnp.transpose(up, (0, 2, 1)).reshape(tr, wd)
    V = pltpu.VMEM
    anyspec = pl.BlockSpec(memory_space=pl.ANY)
    vspec = pl.BlockSpec(memory_space=pltpu.VMEM)
    sspec = pl.BlockSpec(memory_space=pltpu.SMEM)
    width = NY * wd
    scratch = [
        V((NZ, tok, qc), BF16),
        V((2 * NX, tok, width), BF16),
        V((width, qc), BF16),
        V((wd, cols), BF16),
        V((width, RP), BF16),
        V((wd, RP), BF16),
        V((RP, wd), F32),
        V((RP, cols), F32),
        V((RP, qc), F32),
        V((RP, qc), BF16),
        V((NY, 8, qc), F32),
        V((NY, 8, qc), F32),
        V((8, qc), F32),
        V((NZ, 8, qc), F32),
        V((8, qc), F32),
        V((8, qc), F32),
        V((NZ, 8, qc), F32),
        V((8, qc), F32),
        V((RP, qc), F32),
        V((RP, qc), F32),
        V((RP, width), F32),
        V((NZ, 16, qc), F32),
        V((NZ, 16, qc), F32),
        V((NX, tok, width), F32),
        V((NX, tok, width), BF16),
        V((NX, tok, width), BF16),
        V((NX, tok, width), BF16),
        V((NX, tok, width), BF16),
        V((NY, tok, wd), BF16),
        V((NY, tok, wd), BF16),
        V((NY, tr, wd), F32),
        V((NY, tr, wd), F32),
        V((tr, wd), F32),
        V((tr, wd), F32),
        V((tr, wd), F32),
        V((NX, tr, wd), F32),
        V((NY, 8, qc), F32),
        V((tr, qc), F32),
        pltpu.SemaphoreType.DMA((112,)),
        pltpu.SemaphoreType.DMA((112,)),
        pltpu.SemaphoreType.DMA((16,)),
        pltpu.SemaphoreType.DMA((NX,)),
        pltpu.SemaphoreType.DMA((NX,)),
        pltpu.SemaphoreType.DMA((NX,)),
        pltpu.SemaphoreType.DMA((NX,)),
    ]
    dx, mg, dng, upg = pl.pallas_call(
        kernel,
        out_shape=(
            jax.ShapeDtypeStruct((tok, wd), BF16),
            jax.ShapeDtypeStruct((trials, cols), F32),
            jax.ShapeDtypeStruct((tr, cols), F32),
            jax.ShapeDtypeStruct((tr, wd), F32),
        ),
        in_specs=[anyspec, anyspec, anyspec, anyspec, anyspec, vspec, sspec],
        out_specs=(vspec, vspec, anyspec, vspec),
        scratch_shapes=scratch,
        compiler_params=pltpu.CompilerParams(
            collective_id=0, has_side_effects=True, vmem_limit_bytes=56 * 1024 * 1024
        ),
        cost_estimate=pl.CostEstimate(flops=8_000_000_000, bytes_accessed=8_000_000, transcendentals=0),
    )(acts, dy, w, dn, ut, mag, idx)
    return (
        dx,
        mg,
        dng.reshape(trials, rank, cols),
        jnp.transpose(upg.reshape(trials, rank, wd), (0, 2, 1)),
    )


def solution(mesh):
    in_specs = (
        P("col", "row"),
        P("row", "col"),
        P("row", "col"),
        P(None, None, "col"),
        P(None, "row", None),
        P(None, "col"),
        P(),
    )
    out_specs = (P("col", "row"), P(None, "col"), P(None, None, "col"), P(None, "row", None))
    return jax.shard_map(local, mesh=mesh, in_specs=in_specs, out_specs=out_specs, check_vma=False)
```

time: 610 us -> 132 us (0.22); the launches traced: 601 us -> 129 us
  waiting for transfers between devices: 437 us -> 0 us
  matrix products: 131 us -> 0 us
  Pallas kernels: 0 us -> 123 us
  other arithmetic: 14.3 us -> 0 us
  between operations: 14.6 us -> 0.65 us
    psum x3 -> x0, waiting for transfers between devices: 303 us -> none  [the longest x2 239 us: local(): lax.psum((first, k0_part, gram_piece), 'row')]
    dot_general x20 -> x0, matrix products: 131 us -> none  [the longest x1 25 us: local(): dc_term = jnp.dot(hrows.T, dyf * pre, precision=FAST)]
    pallas_call x0 -> x1, Pallas kernels: none -> 123 us  [local(): pl.pallas_call(kernel, out_shape=(jax.ShapeDtypeStruct((tok, wd), BF16),...]
    all_gather x2 -> x0, waiting for transfers between devices: 98.6 us -> none  [the longest x1 98.6 us: local(): piece = lax.all_gather(output_cotangent, 'row', axis=0, tiled=True)]
    reduce_scatter x1 -> x0, waiting for transfers between devices: 34 us -> none  [local(): lax.psum_scatter(dx_acc, 'col', scatter_dimension=0, tiled=True)]
  transfers between devices with their start and end apart: 6 -> 0, of which waited for: 5 -> 0; matrix products, arithmetic and copies ran while one was open for 20% -> 0% of each run, Pallas kernels for 0% -> 0%
where the time goes in v1:
time: 132 us; the launch traced here: 129 us
  Pallas kernels  123 us (93%)
  local copies, waits for them, and re-layouts  5.84 us (4%)
    pallas_call x1, Pallas kernels, local(): pl.pallas_call(kernel, out_shape=(jax.ShapeDtypeStruct((tok, wd), BF16),...  123 us
    unnamed x6, local copies, waits for them, and re-layouts  5.84 us

profile of v1, /device:TPU:8, one launch (start us, length us, event | category | flops | bytes accessed | tf_op | source)
XLA Modules:
  0.0 129.4 jit_solution(1517152200335676448)
XLA Ops:
  0.6 122.9 %shard_map.102 = (bf16[256,256]{1,0:T(8,128)(2,1)}, f32[4,3584]{1,0:T(4,128)}, f32[64,3584]{1,0:T(8,128)}, f32[64,256]{1,0:T(8,128)}) custom-call(bf16[256,256]{1,0:T(8,128)(2,1)} %acts.1, bf16[64,3584]{1,0:T(8,128)(2,1)} %dy.1, bf16[256,3584]{1,0:T(8,128)(2,1)} %w.1, f32[64,3584]{1,0:T(8,128)} %bitcast.10, f32[64,256]{1,0:T(8,128)} %bitcast.11, ...), custom_call_target="tpu_custom_call" | custom-call | flops 8000000000 | bytes 8000000 | tf_op jit(solution)/shard_map/pallas_call | solution.py:439
  123.6 0.0 copy-start
  123.6 1.6 %copy.15 = bf16[256,256]{1,0:T(8,128)(2,1)} copy(bf16[256,256]{1,0:T(8,128)(2,1)} %get-tuple-element.16) | data formatting | bytes 262144
  125.2 1.4 %copy.16 = f32[4,3584]{1,0:T(4,128)} copy(f32[4,3584]{1,0:T(4,128)} %get-tuple-element.17) | data formatting | bytes 114688
  126.6 2.2 %copy.17 = f32[4,16,3584]{2,1,0:T(8,128)} copy(f32[4,16,3584]{2,1,0:T(8,128)} %bitcast.8) | data formatting | bytes 1835008
  128.8 0.0 copy-done
  128.8 0.6 copy.18
Async XLA Ops:
  123.6 5.2 %copy-start = (f32[64,256]{1,0:T(8,128)S(1)}, f32[64,256]{1,0:T(8,128)}, u32[]{:S(2)}) copy-start(f32[64,256]{1,0:T(8,128)} %get-tuple-element.11) | copy-start | bytes 196612

commit v2 on v1

v2 whole, which is shorter than its diff:
```python
import functools

import jax
import jax.numpy as jnp
from jax import lax
from jax.experimental import pallas as pl
from jax.experimental.pallas import tpu as pltpu
from jax.sharding import PartitionSpec as P

SCALE = 2.0
EPS = 1e-06
NX, NY, NZ = 4, 4, 8
MESH = pl.DeviceIdType.MESH
F32, BF16 = jnp.float32, jnp.bfloat16
HP = 512
RP = 128


def mm(a, b, ca, cb, precision=None):
    return lax.dot_general(
        a, b, (((ca,), (cb,)), ((), ())), precision=precision, preferred_element_type=F32
    )


def pack(ref, v):
    n = v.shape[0]
    ref[0:n, :] = v[:, :HP]
    ref[n : 2 * n, 0 : v.shape[1] - HP] = v[:, HP:]


def unpack(p, cols):
    n = p.shape[0] // 2
    return jnp.concatenate([p[:n], p[n:, : cols - HP]], axis=1)


def kernel(
    acts, dy, w, dn, ut, mag, idx,
    out_dx, out_mag, out_dn, out_up,
    dyA, X, Wg, Wo, Ug, Uo, UTs, Df, Dq, Db,
    nyS, nyR, nzS, nzR, resS,
    dsS, dsP, dsR, gfS, qacc, kacc, xpT, qS, qR, kS, kR,
    gpA, pA, dxo, dxs, pairR, xs, xR, ysS, ysR, yfS, yfR, x2S, x2R, acc1,
    upS, upR, upP, upPR, upX, upXR, mgR, dnY,
    ss, rs, ls, ps, pr, xss, xrs, yfs, yfr, x2s, x2r,
):
    row, col = lax.axis_index("row"), lax.axis_index("col")
    z, y = lax.div(row, NY), lax.rem(row, NY)
    x, k = lax.div(col, 2), lax.rem(col, 2)
    rank = 16
    trials = 4
    rows = dy.shape[0]
    cols = w.shape[1]
    qc = cols // NY
    wd = w.shape[0]
    tok = acts.shape[0]
    tr = trials * rank
    hrow = tok // 2

    def mod(v, n):
        return lax.rem(v + n, n)

    def at_y(j):
        return (z * NY + mod(y + j, NY), col)

    def at_z(j):
        return (mod(z + j, NZ) * NY + y, col)

    def at_x(j):
        return (row, mod(x + j, NX) * 2 + k)

    sib = (row, x * 2 + 1 - k)
    YJ = (1, 3, 2)

    barrier = pltpu.get_barrier_semaphore()
    peers = [at_y(j) for j in YJ] + [at_x(j) for j in YJ] + [at_z(j) for j in range(1, NZ)] + [sib]
    for p in peers:
        pl.semaphore_signal(barrier, inc=1, device_id=p, device_id_type=MESH)

    count = [0, 0]
    sent = []

    def remote(src, dst, dev):
        i = count[0]
        count[0] += 1
        d = pltpu.make_async_remote_copy(
            src_ref=src, dst_ref=dst, send_sem=ss.at[i], recv_sem=rs.at[i],
            device_id=dev, device_id_type=MESH,
        )
        d.start()
        sent.append(d)
        return d

    def localcp(src, dst):
        i = count[1]
        count[1] += 1
        d = pltpu.make_async_copy(src, dst, ls.at[i])
        d.start()
        return d

    def yq(j):
        return pl.ds(pl.multiple_of(mod(y + j, NY) * qc, 128), qc)

    yrows = pl.ds(pl.multiple_of(y * rows, rows), rows)
    ywd = pl.ds(pl.multiple_of(y * wd, wd), wd)

    dy_local = localcp(dy.at[:, yq(0)], dyA.at[z, yrows, :])
    ut_local = localcp(ut, UTs.at[pl.ds(0, tr), :])
    wo_local = localcp(w, Wo)
    df_local = localcp(dn, Df.at[pl.ds(0, tr), :])
    act_local = localcp(acts, X.at[col, :, ywd])
    wg_local = localcp(w.at[:, yq(0)], Wg.at[ywd, :])
    UTs[tr:, :] = jnp.zeros((RP - tr, wd), F32)
    Df[tr:, :] = jnp.zeros((RP - tr, cols), F32)
    for ref in (dsS, qacc, xpT):
        ref[...] = jnp.zeros_like(ref)
    pl.semaphore_wait(barrier, len(peers))

    dy_y = [remote(dy.at[:, yq(j)], dyA.at[z, yrows, :], at_y(j)) for j in YJ]
    dy_local.wait()

    def chunk_of(i):
        s = lax.div(i + 1, 2)
        return lax.rem(z + s * (2 * lax.rem(i, 2) - 1) + NZ, NZ)

    def pair_copy(slot):
        return pltpu.make_async_remote_copy(
            src_ref=dxs.at[slot], dst_ref=pairR.at[slot], send_sem=ps.at[slot],
            recv_sem=pr.at[slot], device_id=sib, device_id_type=MESH,
        )

    def x_copy(to, frm):
        return pltpu.make_async_remote_copy(
            src_ref=xs.at[to], dst_ref=xR.at[frm], send_sem=xss.at[to],
            recv_sem=xrs.at[frm], device_id=(row, to * 2 + k), device_id_type=MESH,
        )

    def yf_copy(slot, j):
        return pltpu.make_async_remote_copy(
            src_ref=yfS.at[slot, mod(y + j, NY)], dst_ref=yfR.at[slot, y],
            send_sem=yfs.at[slot, j - 1], recv_sem=yfr.at[slot, j - 1],
            device_id=at_y(j), device_id_type=MESH,
        )

    def x2_copy(to, frm):
        return pltpu.make_async_remote_copy(
            src_ref=x2S.at[to], dst_ref=x2R.at[frm], send_sem=x2s.at[to],
            recv_sem=x2r.at[frm], device_id=(row, to * 2 + k), device_id_type=MESH,
        )

    def trials_of(c):
        t0, t1 = idx[2 * c], idx[2 * c + 1]
        sub = lax.broadcasted_iota(jnp.int32, (tok, RP), 0)
        lane = lax.broadcasted_iota(jnp.int32, (tok, RP), 1)
        return t0, t1, lane // rank == jnp.where(sub < hrow, t0, t1)

    def prep(i, carry):
        c = chunk_of(i)
        t0, t1, mask = trials_of(c)
        dyf = dyA[c].astype(F32)
        res = resS[0:trials, :]
        r0 = jnp.zeros((1, qc), F32)
        r1 = jnp.zeros((1, qc), F32)
        for t in range(trials):
            r0 = jnp.where(t0 == t, res[t : t + 1], r0)
            r1 = jnp.where(t1 == t, res[t : t + 1], r1)
        gpA[c, 0:hrow, :] = (dyf[:hrow] * r0).astype(BF16)
        gpA[c, hrow:, :] = (dyf[hrow:] * r1).astype(BF16)
        pA[c] = jnp.where(mask, mm(gpA[c], Db[...], 1, 1), 0.0).astype(BF16)
        return carry

    ring = {}

    def zstep(step, b):
        ys = mod(y - (0, 1, 3, 2)[b], NY)
        brows = pl.ds(pl.multiple_of(ys * rows, rows), rows)
        for sign in (1, -1):
            if step > 1:
                ring[sign, step - 1, b].wait_recv()
            if step < 4 or (b < 2) == (sign == 1):
                src = dyA.at[mod(z - sign * (step - 1), NZ), brows, :]
                ring[sign, step, b] = remote(src, src, at_z(sign))

    zstep(1, 0)
    act_y = [remote(acts, X.at[col, :, ywd], at_y(j)) for j in YJ]
    ut_local.wait()
    Uo[...] = UTs[...].T.astype(BF16)
    u_local = localcp(Uo, Ug.at[ywd, :])
    df_local.wait()
    wo_local.wait()

    def norm_piece(yy):
        for h, (c0, n) in enumerate(((0, HP), (HP, qc - HP))):
            at = slice(yy * qc + c0, yy * qc + c0 + n)
            wb = Wo[:, at].astype(F32)
            db = (SCALE * Df[:, at]).astype(BF16)
            owner = lax.broadcasted_iota(jnp.int32, db.shape, 0) // rank
            for t in range(trials):
                m = wb + mm(Uo[...], jnp.where(owner == t, db, jnp.zeros_like(db)), 1, 0)
                r = h * trials + t
                nyS[yy, r : r + 1, 0:n] = jnp.sum(m * m, axis=0, keepdims=True)

    norm_piece(0)
    norm_piece(1)
    for b, d in enumerate(dy_y):
        d.wait_recv()
        zstep(1, b + 1)
    u_y = [remote(Uo, Ug.at[ywd, :], at_y(j)) for j in YJ]
    norm_piece(2)
    norm_piece(3)
    ny_y = [remote(nyS.at[mod(y + j, NY)], nyR.at[y], at_y(j)) for j in YJ]
    zstep(2, 0)
    zstep(2, 1)

    act_local.wait()
    for d in act_y:
        d.wait_recv()
    w_y = [remote(w.at[:, yq(j)], Wg.at[ywd, :], at_y(j)) for j in YJ]
    h0, h1 = pl.ds(0, hrow), pl.ds(hrow, hrow)

    def xpart(j, h):
        return X.at[mod(x + j, NX) * 2 + k, h, :]

    def xwhole(j):
        return X.at[mod(x + j, NX) * 2 + k]

    xp = [remote(xpart(0, h), xpart(0, h), at_x(1)) for h in (h0, h1)]
    xm = [remote(xpart(0, h), xpart(0, h), at_x(-1)) for h in (h1, h0)]
    x_sib = [remote(xwhole(0), xwhole(0), sib)]
    zstep(2, 2)
    for d in ny_y:
        d.wait_recv()
    nzS[...] = nyS[y] + nyR[mod(y + 1, NY)] + nyR[mod(y + 2, NY)] + nyR[mod(y + 3, NY)]
    nz_z = [remote(nzS, nzR.at[z], at_z(j)) for j in range(1, NZ)]
    zstep(2, 3)
    zstep(3, 0)
    zstep(3, 1)
    xp[0].wait_recv()
    xp.append(remote(xpart(-1, h0), xpart(-1, h0), at_x(1)))
    xm[0].wait_recv()
    xm.append(remote(xpart(1, h1), xpart(1, h1), at_x(-1)))
    Dq[...] = Df[:, pl.ds(pl.multiple_of(y * qc, 128), qc)]
    Db[...] = Dq[...].astype(BF16)
    zstep(3, 2)
    for d in nz_z:
        d.wait_recv()
    nsq = nzS[...]
    for j in range(1, NZ):
        nsq = nsq + nzR[mod(z + j, NZ)]
    norm = jnp.sqrt(unpack(nsq, qc) + EPS)
    magq = mag[:, pl.ds(pl.multiple_of(y * qc, 128), qc)]
    resS[0:trials, :] = magq / norm
    zstep(3, 3)
    xp[1].wait_recv()
    xm[1].wait_recv()
    x_sib += [remote(xwhole(j), xwhole(j), sib) for j in (-1, 1)]
    zstep(4, 0)
    lax.fori_loop(0, 5, prep, 0)
    zstep(4, 1)
    xp[2].wait_recv()
    xm[2].wait_recv()
    x_sib.append(remote(xwhole(2), xwhole(2), sib))
    zstep(4, 2)
    zstep(4, 3)
    lax.fori_loop(5, NZ - 1, prep, 0)
    u_local.wait()
    wg_local.wait()
    for d in u_y + w_y:
        d.wait_recv()

    same = (
        lax.broadcasted_iota(jnp.int32, (RP, RP), 0) // rank
        == lax.broadcasted_iota(jnp.int32, (RP, RP), 1) // rank
    )
    gram = jnp.where(same, mm(Ug[...], Ug[...], 0, 0), 0.0)
    kacc[...] = mm(Ug[...], Wg[...], 0, 0) + SCALE * mm(gram.astype(BF16), Db[...], 1, 0)
    for zz in range(NZ):
        pack(kS.at[zz], kacc[8 * zz : 8 * zz + 8, :].astype(BF16))
    k_z = [remote(kS.at[mod(z + j, NZ)], kR.at[z], at_z(j)) for j in range(1, NZ)]
    for d in x_sib:
        d.wait_recv()

    def scales(c):
        t0, t1, mask = trials_of(c)
        xc = X[c]
        dyc = dyA[c]
        q = jnp.where(mask, mm(xc, Ug[...], 1, 0), 0.0).astype(BF16)
        pre = mm(xc, Wg[...], 1, 0) + SCALE * mm(q, Db[...], 1, 0)
        e = dyc.astype(F32) * pre
        trow = lax.broadcasted_iota(jnp.int32, (8, qc), 0)
        s0 = jnp.sum(e[:hrow], axis=0, keepdims=True)
        s1 = jnp.sum(e[hrow:], axis=0, keepdims=True)
        dsS[...] += jnp.where(trow == t0, s0, 0.0) + jnp.where(trow == t1, s1, 0.0)
        qacc[...] += mm(q, dyc, 0, 0)

    def inputs(c):
        p = pA[c]
        xpT[...] += mm(p, X[c], 0, 0)
        dx = mm(gpA[c], Wg[...], 1, 1) + SCALE * mm(p, Ug[...], 1, 1)
        slot = lax.div(c, 2)

        @pl.when(lax.rem(c, 2) == k)
        def _():
            dxo[slot] = dx

        @pl.when(lax.rem(c, 2) != k)
        def _():
            dxs[slot] = dx.astype(BF16)
            pair_copy(slot).start()

    def pass_on(i):
        c = chunk_of(i)
        slot = lax.div(c, 2)

        @pl.when(lax.rem(c, 2) == k)
        def _():
            pair_copy(slot).wait_recv()
            total = dxo[slot] + pairR[slot].astype(F32)
            dxo[slot] = total

            @pl.when(slot != x)
            def _():
                xs[slot] = total[:hrow].astype(BF16)
                x_copy(slot, x).start()

            for yy in range(NY):
                yfS[slot, yy] = total[hrow:, yy * wd : (yy + 1) * wd].astype(BF16)
            for j in YJ:
                yf_copy(slot, j).start()

    def pass_twice(i):
        c = chunk_of(i)
        slot = lax.div(c, 2)

        @pl.when(lax.rem(c, 2) == k)
        def _():
            for j in YJ:
                yf_copy(slot, j).wait_recv()
            total = dxo[slot, hrow:, ywd]
            for j in (1, 2, 3):
                total = total + yfR[slot, mod(y + j, NY)].astype(F32)

            @pl.when(slot == x)
            def _():
                acc1[...] = total

            @pl.when(slot != x)
            def _():
                x2S[slot] = total.astype(BF16)
                x2_copy(slot, x).start()

    def step(i, carry):
        c = chunk_of(i)
        inputs(c)
        scales(c)

        @pl.when(i > 0)
        def _():
            pass_on(i - 1)

        @pl.when(i > 3)
        def _():
            pass_twice(i - 4)

        return carry

    lax.fori_loop(0, NZ - 1, step, 0)
    for key in ((1, 4, 0), (1, 4, 1), (-1, 4, 2), (-1, 4, 3)):
        ring[key].wait_recv()
    last = chunk_of(NZ - 1)
    scales(last)

    pack(dsP, dsS[0:trials, :])
    ds_z = [remote(dsP, dsR.at[z], at_z(j)) for j in range(1, NZ)]
    for zz in range(NZ):
        pack(qS.at[zz], qacc[8 * zz : 8 * zz + 8, :].astype(BF16))
    q_z = [remote(qS.at[mod(z + j, NZ)], qR.at[z], at_z(j)) for j in range(1, NZ)]
    prep(NZ - 1, 0)
    inputs(last)
    pass_on(NZ - 2)
    pass_twice(NZ - 5)
    pass_on(NZ - 1)
    for d in ds_z:
        d.wait_recv()
    dsum = dsP[...]
    for j in range(1, NZ):
        dsum = dsum + dsR[mod(z + j, NZ)]
    dsum = unpack(dsum, qc)
    pack(mgR.at[y], dsum / norm)
    mg_y = [remote(mgR.at[y], mgR.at[y], at_y(j)) for j in YJ]
    gf = -dsum * magq / (norm * norm * norm)
    gfS[0:trials, :] = gf
    dg = jnp.concatenate(
        [Dq[rank * t : rank * (t + 1), :] * gf[t : t + 1] for t in range(trials)]
        + [jnp.zeros((RP - tr, qc), F32)],
        axis=0,
    ).astype(BF16)
    inner = jnp.where(same, mm(dg, Db[...], 1, 1), 0.0).astype(BF16)
    up = SCALE * (xpT[...] + mm(dg, Wg[...], 1, 1) + SCALE * mm(inner, Ug[...], 1, 1))
    for yy in range(NY):
        upS[yy] = up[:tr, yy * wd : (yy + 1) * wd]
    up_y = [remote(upS.at[mod(y + j, NY)], upR.at[y], at_y(j)) for j in YJ]

    pass_twice(NZ - 4)
    pass_twice(NZ - 3)
    for d in k_z + q_z:
        d.wait_recv()
    zrows = pl.ds(pl.multiple_of(z * 8, 8), 8)
    qsum = qR[mod(z + 1, NZ)].astype(F32)
    ksum = kR[mod(z + 1, NZ)].astype(F32)
    for j in range(2, NZ):
        qsum = qsum + qR[mod(z + j, NZ)].astype(F32)
        ksum = ksum + kR[mod(z + j, NZ)].astype(F32)
    qsum = unpack(qsum, qc) + qacc[zrows, :]
    ksum = unpack(ksum, qc) + kacc[zrows, :]
    tz = lax.div(z * 8, rank)
    pack(
        dnY.at[y, z],
        (SCALE * (qsum * resS[pl.ds(tz, 1), :] + ksum * gfS[pl.ds(tz, 1), :])).astype(BF16),
    )
    dn_z = [remote(dnY.at[y, z], dnY.at[y, z], at_z(j)) for j in range(1, NZ)]

    pass_twice(NZ - 2)
    for d in up_y:
        d.wait_recv()
    upP[...] = upS[y] + upR[mod(y + 1, NY)] + upR[mod(y + 2, NY)] + upR[mod(y + 3, NY)]
    up_p = remote(upP, upPR, sib)

    pass_twice(NZ - 1)
    for d in dn_z:
        d.wait_recv()
    dn_y = [remote(dnY.at[y], dnY.at[y], at_y(j)) for j in YJ]

    up_p.wait_recv()
    upX[...] = upP[...] + upPR[...]
    up_x = [remote(upX, upXR.at[x], at_x(j)) for j in YJ]

    for j in (1, 2, 3):
        x_copy(mod(x + j, NX), mod(x + j, NX)).wait_recv()
    total = dxo[x, 0:hrow, :]
    for j in (1, 2, 3):
        total = total + xR[mod(x + j, NX)].astype(F32)
    dxo[x, 0:hrow, :] = total
    for yy in range(NY):
        ysS[yy] = total[:, yy * wd : (yy + 1) * wd].astype(BF16)
    ys_y = [remote(ysS.at[mod(y + j, NY)], ysR.at[y], at_y(j)) for j in YJ]

    for d in up_x:
        d.wait_recv()
    out_up[...] = upX[...] + upXR[mod(x + 1, NX)] + upXR[mod(x + 2, NX)] + upXR[mod(x + 3, NX)]
    for d in mg_y:
        d.wait_recv()
    out_mag[...] = mgR[...]
    for d in ys_y:
        d.wait_recv()
    acc = dxo[x, 0:hrow, ywd]
    for j in (1, 2, 3):
        acc = acc + ysR[mod(y + j, NY)].astype(F32)
    out_dx[0:hrow, :] = acc.astype(BF16)
    for j in (1, 2, 3):
        x2_copy(mod(x + j, NX), mod(x + j, NX)).wait_recv()
    acc = acc1[...]
    for j in (1, 2, 3):
        acc = acc + x2R[mod(x + j, NX)].astype(F32)
    out_dx[hrow:, :] = acc.astype(BF16)

    for d in dn_y:
        d.wait_recv()
    out_dn[...] = dnY[...]
    for d in sent:
        d.wait_send()
    for slot in range(NX):
        pair_copy(slot).wait_send()
        for j in YJ:
            yf_copy(slot, j).wait_send()
    for j in (1, 2, 3):
        x_copy(mod(x + j, NX), x).wait_send()
        x2_copy(mod(x + j, NX), x).wait_send()


def write_out(dx, mg, dnp, up, o_dx, o_mag, o_dn, o_up):
    o_dx[...] = dx[...]
    o_up[...] = up[...]
    trials, cols = o_mag.shape
    qc = cols // NY
    for yy in range(NY):
        o_mag[:, yy * qc : (yy + 1) * qc] = unpack(mg[yy], qc)
        for zz in range(NZ):
            o_dn[8 * zz : 8 * zz + 8, yy * qc : (yy + 1) * qc] = unpack(dnp[yy, zz].astype(F32), qc)


def local(acts, dy, w, down, up, mag, idx):
    trials, rank, cols = down.shape
    wd = w.shape[0]
    tok = acts.shape[0]
    qc = cols // NY
    tr = trials * rank
    dn = down.reshape(tr, cols)
    ut = jnp.transpose(up, (0, 2, 1)).reshape(tr, wd)
    V = pltpu.VMEM
    anyspec = pl.BlockSpec(memory_space=pl.ANY)
    vspec = pl.BlockSpec(memory_space=pltpu.VMEM)
    sspec = pl.BlockSpec(memory_space=pltpu.SMEM)
    width = NY * wd
    scratch = [
        V((NZ, tok, qc), BF16),
        V((2 * NX, tok, width), BF16),
        V((width, qc), BF16),
        V((wd, cols), BF16),
        V((width, RP), BF16),
        V((wd, RP), BF16),
        V((RP, wd), F32),
        V((RP, cols), F32),
        V((RP, qc), F32),
        V((RP, qc), BF16),
        V((NY, 8, HP), F32),
        V((NY, 8, HP), F32),
        V((8, HP), F32),
        V((NZ, 8, HP), F32),
        V((8, qc), F32),
        V((8, qc), F32),
        V((8, HP), F32),
        V((NZ, 8, HP), F32),
        V((8, qc), F32),
        V((RP, qc), F32),
        V((RP, qc), F32),
        V((RP, width), F32),
        V((NZ, 16, HP), BF16),
        V((NZ, 16, HP), BF16),
        V((NZ, 16, HP), BF16),
        V((NZ, 16, HP), BF16),
        V((NZ, tok, qc), BF16),
        V((NZ, tok, RP), BF16),
        V((NX, tok, width), F32),
        V((NX, tok, width), BF16),
        V((NX, tok, width), BF16),
        V((NX, tok // 2, width), BF16),
        V((NX, tok // 2, width), BF16),
        V((NY, tok // 2, wd), BF16),
        V((NY, tok // 2, wd), BF16),
        V((NX, NY, tok // 2, wd), BF16),
        V((NX, NY, tok // 2, wd), BF16),
        V((NX, tok // 2, wd), BF16),
        V((NX, tok // 2, wd), BF16),
        V((tok // 2, wd), F32),
        V((NY, tr, wd), F32),
        V((NY, tr, wd), F32),
        V((tr, wd), F32),
        V((tr, wd), F32),
        V((tr, wd), F32),
        V((NX, tr, wd), F32),
        V((NY, 8, HP), F32),
        V((NY, NZ, 16, HP), BF16),
        pltpu.SemaphoreType.DMA((112,)),
        pltpu.SemaphoreType.DMA((112,)),
        pltpu.SemaphoreType.DMA((16,)),
        pltpu.SemaphoreType.DMA((NX,)),
        pltpu.SemaphoreType.DMA((NX,)),
        pltpu.SemaphoreType.DMA((NX,)),
        pltpu.SemaphoreType.DMA((NX,)),
        pltpu.SemaphoreType.DMA((NX, 3)),
        pltpu.SemaphoreType.DMA((NX, 3)),
        pltpu.SemaphoreType.DMA((NX,)),
        pltpu.SemaphoreType.DMA((NX,)),
    ]
    dx, mg, dng, upg = pl.pallas_call(
        kernel,
        out_shape=(
            jax.ShapeDtypeStruct((tok, wd), BF16),
            jax.ShapeDtypeStruct((NY, 8, HP), F32),
            jax.ShapeDtypeStruct((NY, NZ, 16, HP), BF16),
            jax.ShapeDtypeStruct((tr, wd), F32),
        ),
        in_specs=[anyspec, anyspec, anyspec, anyspec, anyspec, vspec, sspec],
        out_specs=(vspec,) * 4,
        scratch_shapes=scratch,
        compiler_params=pltpu.CompilerParams(
            collective_id=0, has_side_effects=True, vmem_limit_bytes=56 * 1024 * 1024
        ),
        cost_estimate=pl.CostEstimate(flops=8_000_000_000, bytes_accessed=8_000_000, transcendentals=0),
    )(acts, dy, w, dn, ut, mag, idx)
    dx, mg, dng, upg = pl.pallas_call(
        write_out,
        out_shape=(
            jax.ShapeDtypeStruct((tok, wd), BF16),
            jax.ShapeDtypeStruct((trials, cols), F32),
            jax.ShapeDtypeStruct((tr, cols), F32),
            jax.ShapeDtypeStruct((tr, wd), F32),
        ),
        in_specs=[vspec] * 4,
        out_specs=(vspec,) * 4,
    )(dx, mg, dng, upg)
    return (
        dx,
        mg,
        dng.reshape(trials, rank, cols),
        jnp.transpose(upg.reshape(trials, rank, wd), (0, 2, 1)),
    )


def solution(mesh):
    in_specs = (
        P("col", "row"),
        P("row", "col"),
        P("row", "col"),
        P(None, None, "col"),
        P(None, "row", None),
        P(None, "col"),
        P(),
    )
    out_specs = (P("col", "row"), P(None, "col"), P(None, None, "col"), P(None, "row", None))
    return jax.shard_map(local, mesh=mesh, in_specs=in_specs, out_specs=out_specs, check_vma=False)
```

time: 132 us -> 94.8 us (0.72)
  Pallas kernels: 123 us -> 92.4 us
  local copies, waits for them, and re-layouts: 5.84 us -> 0 us
    pallas_call x1, Pallas kernels: 123 us -> 90.2 us  [local(): pl.pallas_call(kernel, out_shape=(jax.ShapeDtypeStruct((tok, wd), BF16),...]
    unnamed x6 -> x0, local copies, waits for them, and re-layouts: 5.84 us -> none
    pallas_call x0 -> x1, Pallas kernels: none -> 2.17 us  [local(): pl.pallas_call(write_out, out_shape=(jax.ShapeDtypeStruct((tok, wd), BF16...]
where the time goes in v2:
time: 94.8 us; the launch traced here: 93 us
  Pallas kernels  92.4 us (97%)
    pallas_call x1, Pallas kernels, local(): pl.pallas_call(kernel, out_shape=(jax.ShapeDtypeStruct((tok, wd), BF16),...  90.2 us
    pallas_call x1, Pallas kernels, local(): pl.pallas_call(write_out, out_shape=(jax.ShapeDtypeStruct((tok, wd), BF16...  2.17 us

profile of v2, /device:TPU:8, one launch (start us, length us, event | category | flops | bytes accessed | tf_op | source)
XLA Modules:
  0.0 93.0 jit_solution(11963211200042437491)
XLA Ops:
  0.6 90.2 %shard_map.102 = (bf16[256,256]{1,0:T(8,128)(2,1)}, f32[4,8,512]{2,1,0:T(8,128)}, bf16[4,8,16,512]{3,2,1,0:T(8,128)(2,1)}, f32[64,256]{1,0:T(8,128)}) custom-call(bf16[256,256]{1,0:T(8,128)(2,1)} %acts.1, bf16[64,3584]{1,0:T(8,128)(2,1)} %dy.1, bf16[256,3584]{1,0:T(8,128)(2,1)} %w.1, f32[64,3584]{1,0:T(8,128)} %bitcast.8, f32[64,256]{1,0:T(8,128)} %bitcast.10, ...), custom_call_target="tpu_custom_call" | custom-call | flops 8000000000 | bytes 8000000 | tf_op jit(solution)/shard_map/pallas_call | solution.py:565
  90.8 2.2 %shard_map.103 = (bf16[256,256]{1,0:T(8,128)(2,1)}, f32[4,3584]{1,0:T(4,128)}, f32[64,3584]{1,0:T(8,128)}, f32[64,256]{1,0:T(8,128)}) custom-call(bf16[256,256]{1,0:T(8,128)(2,1)} %get-tuple-element.12.dx, f32[4,8,512]{2,1,0:T(8,128)} %get-tuple-element.13.mg, bf16[4,8,16,512]{3,2,1,0:T(8,128)(2,1)} %get-tuple-element.14.dnp, f32[64,256]{1,0:T(8,128)} %get-tuple-element.15.up), custom_call_target="tpu_custom_call" | custom-call | tf_op jit(solution)/shard_map/pallas_call | solution.py:581

commit v3 on v2

--- a/solution.py
+++ b/solution.py
@@ -40,7 +40,7 @@
     nyS, nyR, nzS, nzR, resS,
     dsS, dsP, dsR, gfS, qacc, kacc, xpT, qS, qR, kS, kR,
     gpA, pA, dxo, dxs, pairR, xs, xR, ysS, ysR, yfS, yfR, x2S, x2R, acc1,
-    upS, upR, upP, upPR, upX, upXR, mgR, dnY,
+    upS, upR, upX, upXR, mgR, dnY,
     ss, rs, ls, ps, pr, xss, xrs, yfs, yfr, x2s, x2r,
 ):
     row, col = lax.axis_index("row"), lax.axis_index("col")
@@ -72,7 +72,9 @@
     YJ = (1, 3, 2)
 
     barrier = pltpu.get_barrier_semaphore()
-    peers = [at_y(j) for j in YJ] + [at_x(j) for j in YJ] + [at_z(j) for j in range(1, NZ)] + [sib]
+    others = [(row, mod(x + j, NX) * 2 + 1 - k) for j in (1, 2, 3)]
+    peers = [at_y(j) for j in YJ] + [at_x(j) for j in YJ] + [at_z(j) for j in range(1, NZ)]
+    peers += others + [sib]
     for p in peers:
         pl.semaphore_signal(barrier, inc=1, device_id=p, device_id_type=MESH)
 
@@ -168,116 +170,9 @@
         pA[c] = jnp.where(mask, mm(gpA[c], Db[...], 1, 1), 0.0).astype(BF16)
         return carry
 
-    ring = {}
-
-    def zstep(step, b):
-        ys = mod(y - (0, 1, 3, 2)[b], NY)
-        brows = pl.ds(pl.multiple_of(ys * rows, rows), rows)
-        for sign in (1, -1):
-            if step > 1:
-                ring[sign, step - 1, b].wait_recv()
-            if step < 4 or (b < 2) == (sign == 1):
-                src = dyA.at[mod(z - sign * (step - 1), NZ), brows, :]
-                ring[sign, step, b] = remote(src, src, at_z(sign))
-
-    zstep(1, 0)
-    act_y = [remote(acts, X.at[col, :, ywd], at_y(j)) for j in YJ]
-    ut_local.wait()
-    Uo[...] = UTs[...].T.astype(BF16)
-    u_local = localcp(Uo, Ug.at[ywd, :])
-    df_local.wait()
-    wo_local.wait()
-
-    def norm_piece(yy):
-        for h, (c0, n) in enumerate(((0, HP), (HP, qc - HP))):
-            at = slice(yy * qc + c0, yy * qc + c0 + n)
-            wb = Wo[:, at].astype(F32)
-            db = (SCALE * Df[:, at]).astype(BF16)
-            owner = lax.broadcasted_iota(jnp.int32, db.shape, 0) // rank
-            for t in range(trials):
-                m = wb + mm(Uo[...], jnp.where(owner == t, db, jnp.zeros_like(db)), 1, 0)
-                r = h * trials + t
-                nyS[yy, r : r + 1, 0:n] = jnp.sum(m * m, axis=0, keepdims=True)
-
-    norm_piece(0)
-    norm_piece(1)
-    for b, d in enumerate(dy_y):
-        d.wait_recv()
-        zstep(1, b + 1)
-    u_y = [remote(Uo, Ug.at[ywd, :], at_y(j)) for j in YJ]
-    norm_piece(2)
-    norm_piece(3)
-    ny_y = [remote(nyS.at[mod(y + j, NY)], nyR.at[y], at_y(j)) for j in YJ]
-    zstep(2, 0)
-    zstep(2, 1)
-
-    act_local.wait()
-    for d in act_y:
-        d.wait_recv()
-    w_y = [remote(w.at[:, yq(j)], Wg.at[ywd, :], at_y(j)) for j in YJ]
-    h0, h1 = pl.ds(0, hrow), pl.ds(hrow, hrow)
-
-    def xpart(j, h):
-        return X.at[mod(x + j, NX) * 2 + k, h, :]
-
-    def xwhole(j):
-        return X.at[mod(x + j, NX) * 2 + k]
-
-    xp = [remote(xpart(0, h), xpart(0, h), at_x(1)) for h in (h0, h1)]
-    xm = [remote(xpart(0, h), xpart(0, h), at_x(-1)) for h in (h1, h0)]
-    x_sib = [remote(xwhole(0), xwhole(0), sib)]
-    zstep(2, 2)
-    for d in ny_y:
-        d.wait_recv()
-    nzS[...] = nyS[y] + nyR[mod(y + 1, NY)] + nyR[mod(y + 2, NY)] + nyR[mod(y + 3, NY)]
-    nz_z = [remote(nzS, nzR.at[z], at_z(j)) for j in range(1, NZ)]
-    zstep(2, 3)
-    zstep(3, 0)
-    zstep(3, 1)
-    xp[0].wait_recv()
-    xp.append(remote(xpart(-1, h0), xpart(-1, h0), at_x(1)))
-    xm[0].wait_recv()
-    xm.append(remote(xpart(1, h1), xpart(1, h1), at_x(-1)))
-    Dq[...] = Df[:, pl.ds(pl.multiple_of(y * qc, 128), qc)]
-    Db[...] = Dq[...].astype(BF16)
-    zstep(3, 2)
-    for d in nz_z:
-        d.wait_recv()
-    nsq = nzS[...]
-    for j in range(1, NZ):
-        nsq = nsq + nzR[mod(z + j, NZ)]
-    norm = jnp.sqrt(unpack(nsq, qc) + EPS)
-    magq = mag[:, pl.ds(pl.multiple_of(y * qc, 128), qc)]
-    resS[0:trials, :] = magq / norm
-    zstep(3, 3)
-    xp[1].wait_recv()
-    xm[1].wait_recv()
-    x_sib += [remote(xwhole(j), xwhole(j), sib) for j in (-1, 1)]
-    zstep(4, 0)
-    lax.fori_loop(0, 5, prep, 0)
-    zstep(4, 1)
-    xp[2].wait_recv()
-    xm[2].wait_recv()
-    x_sib.append(remote(xwhole(2), xwhole(2), sib))
-    zstep(4, 2)
-    zstep(4, 3)
-    lax.fori_loop(5, NZ - 1, prep, 0)
-    u_local.wait()
-    wg_local.wait()
-    for d in u_y + w_y:
-        d.wait_recv()
-
-    same = (
-        lax.broadcasted_iota(jnp.int32, (RP, RP), 0) // rank
-        == lax.broadcasted_iota(jnp.int32, (RP, RP), 1) // rank
-    )
-    gram = jnp.where(same, mm(Ug[...], Ug[...], 0, 0), 0.0)
-    kacc[...] = mm(Ug[...], Wg[...], 0, 0) + SCALE * mm(gram.astype(BF16), Db[...], 1, 0)
-    for zz in range(NZ):
-        pack(kS.at[zz], kacc[8 * zz : 8 * zz + 8, :].astype(BF16))
-    k_z = [remote(kS.at[mod(z + j, NZ)], kR.at[z], at_z(j)) for j in range(1, NZ)]
-    for d in x_sib:
-        d.wait_recv()
+    def kpart(yb):
+        brows = pl.ds(pl.multiple_of(yb * wd, wd), wd)
+        kacc[...] += mm(Ug[brows, :], Wg[brows, :], 0, 0)
 
     def scales(c):
         t0, t1, mask = trials_of(c)
@@ -292,10 +187,10 @@
         dsS[...] += jnp.where(trow == t0, s0, 0.0) + jnp.where(trow == t1, s1, 0.0)
         qacc[...] += mm(q, dyc, 0, 0)
 
-    def inputs(c):
-        p = pA[c]
-        xpT[...] += mm(p, X[c], 0, 0)
-        dx = mm(gpA[c], Wg[...], 1, 1) + SCALE * mm(p, Ug[...], 1, 1)
+    def inputs(i, carry):
+        c = chunk_of(i)
+        xpT[...] += mm(pA[c], X[c], 0, 0)
+        dx = mm(gpA[c], Wg[...], 1, 1) + SCALE * mm(pA[c], Ug[...], 1, 1)
         slot = lax.div(c, 2)
 
         @pl.when(lax.rem(c, 2) == k)
@@ -306,6 +201,8 @@
         def _():
             dxs[slot] = dx.astype(BF16)
             pair_copy(slot).start()
+
+        return carry
 
     def pass_on(i):
         c = chunk_of(i)
@@ -348,10 +245,125 @@
                 x2S[slot] = total.astype(BF16)
                 x2_copy(slot, x).start()
 
+    ring = {}
+
+    def zstep(step, b):
+        ys = mod(y - (0, 1, 3, 2)[b], NY)
+        brows = pl.ds(pl.multiple_of(ys * rows, rows), rows)
+        for sign in (1, -1):
+            if step > 1:
+                ring[sign, step - 1, b].wait_recv()
+            if step < 4 or (b < 2) == (sign == 1):
+                src = dyA.at[mod(z - sign * (step - 1), NZ), brows, :]
+                ring[sign, step, b] = remote(src, src, at_z(sign))
+
+    zstep(1, 0)
+    act_y = [remote(acts, X.at[col, :, ywd], at_y(j)) for j in YJ]
+    ut_local.wait()
+    Uo[...] = UTs[...].T.astype(BF16)
+    u_local = localcp(Uo, Ug.at[ywd, :])
+    df_local.wait()
+    wo_local.wait()
+
+    def norm_piece(yy):
+        for h, (c0, n) in enumerate(((0, HP), (HP, qc - HP))):
+            at = slice(yy * qc + c0, yy * qc + c0 + n)
+            wb = Wo[:, at].astype(F32)
+            db = (SCALE * Df[:, at]).astype(BF16)
+            owner = lax.broadcasted_iota(jnp.int32, db.shape, 0) // rank
+            for t in range(trials):
+                m = wb + mm(Uo[...], jnp.where(owner == t, db, jnp.zeros_like(db)), 1, 0)
+                r = h * trials + t
+                nyS[yy, r : r + 1, 0:n] = jnp.sum(m * m, axis=0, keepdims=True)
+
+    for yy in range(NY):
+        norm_piece(yy)
+    ny_y = [remote(nyS.at[mod(y + j, NY)], nyR.at[y], at_y(j)) for j in YJ]
+    u_y = [remote(Uo, Ug.at[ywd, :], at_y(j)) for j in YJ]
+    for b, d in enumerate(dy_y):
+        d.wait_recv()
+        zstep(1, b + 1)
+    Dq[...] = Df[:, pl.ds(pl.multiple_of(y * qc, 128), qc)]
+    Db[...] = Dq[...].astype(BF16)
+    zstep(2, 0)
+    for d in ny_y:
+        d.wait_recv()
+    nzS[...] = nyS[y] + nyR[mod(y + 1, NY)] + nyR[mod(y + 2, NY)] + nyR[mod(y + 3, NY)]
+    nz_z = [remote(nzS, nzR.at[z], at_z(j)) for j in range(1, NZ)]
+    zstep(2, 1)
+
+    act_local.wait()
+    for d in act_y:
+        d.wait_recv()
+    w_y = [remote(w.at[:, yq(j)], Wg.at[ywd, :], at_y(j)) for j in YJ]
+    h0, h1 = pl.ds(0, hrow), pl.ds(hrow, hrow)
+
+    def xpart(j, h):
+        return X.at[mod(x + j, NX) * 2 + k, h, :]
+
+    def xwhole(j):
+        return X.at[mod(x + j, NX) * 2 + k]
+
+    xp = [remote(xpart(0, h), xpart(0, h), at_x(1)) for h in (h0, h1)]
+    xm = [remote(xpart(0, h), xpart(0, h), at_x(-1)) for h in (h1, h0)]
+    x_sib = [remote(xwhole(0), xwhole(0), sib)]
+    zstep(2, 2)
+    zstep(2, 3)
+    for d in nz_z:
+        d.wait_recv()
+    nsq = nzS[...]
+    for j in range(1, NZ):
+        nsq = nsq + nzR[mod(z + j, NZ)]
+    norm = jnp.sqrt(unpack(nsq, qc) + EPS)
+    magq = mag[:, pl.ds(pl.multiple_of(y * qc, 128), qc)]
+    resS[0:trials, :] = magq / norm
+    zstep(3, 0)
+
+    u_local.wait()
+    for d in u_y:
+        d.wait_recv()
+    same = (
+        lax.broadcasted_iota(jnp.int32, (RP, RP), 0) // rank
+        == lax.broadcasted_iota(jnp.int32, (RP, RP), 1) // rank
+    )
+    gram = jnp.where(same, mm(Ug[...], Ug[...], 0, 0), 0.0)
+    kacc[...] = SCALE * mm(gram.astype(BF16), Db[...], 1, 0)
+    wg_local.wait()
+    kpart(y)
+    lax.fori_loop(0, 3, prep, 0)
+    zstep(3, 1)
+    xp[0].wait_recv()
+    xp.append(remote(xpart(-1, h0), xpart(-1, h0), at_x(1)))
+    xm[0].wait_recv()
+    xm.append(remote(xpart(1, h1), xpart(1, h1), at_x(-1)))
+    zstep(3, 2)
+    zstep(3, 3)
+    xp[1].wait_recv()
+    xm[1].wait_recv()
+    x_sib += [remote(xwhole(j), xwhole(j), sib) for j in (-1, 1)]
+    zstep(4, 0)
+    lax.fori_loop(3, 5, prep, 0)
+    zstep(4, 1)
+    xp[2].wait_recv()
+    xm[2].wait_recv()
+    x_sib.append(remote(xwhole(2), xwhole(2), sib))
+    zstep(4, 2)
+    for j, d in zip((1, 3), w_y):
+        d.wait_recv()
+        kpart(mod(y - j, NY))
+    zstep(4, 3)
+    lax.fori_loop(5, NZ - 1, prep, 0)
+    w_y[2].wait_recv()
+    kpart(mod(y - 2, NY))
+    for zz in range(NZ):
+        pack(kS.at[zz], kacc[8 * zz : 8 * zz + 8, :].astype(BF16))
+    k_z = [remote(kS.at[mod(z + j, NZ)], kR.at[z], at_z(j)) for j in range(1, NZ)]
+    for d in x_sib:
+        d.wait_recv()
+
     def step(i, carry):
-        c = chunk_of(i)
-        inputs(c)
-        scales(c)
+        inputs(i, carry)
+        scales(chunk_of(i))
 
         @pl.when(i > 0)
         def _():
@@ -368,16 +380,17 @@
         ring[key].wait_recv()
     last = chunk_of(NZ - 1)
     scales(last)
-
     pack(dsP, dsS[0:trials, :])
     ds_z = [remote(dsP, dsR.at[z], at_z(j)) for j in range(1, NZ)]
     for zz in range(NZ):
         pack(qS.at[zz], qacc[8 * zz : 8 * zz + 8, :].astype(BF16))
     q_z = [remote(qS.at[mod(z + j, NZ)], qR.at[z], at_z(j)) for j in range(1, NZ)]
+
     prep(NZ - 1, 0)
-    inputs(last)
+    inputs(NZ - 1, 0)
     pass_on(NZ - 2)
     pass_twice(NZ - 5)
+    pass_twice(NZ - 4)
     pass_on(NZ - 1)
     for d in ds_z:
         d.wait_recv()
@@ -385,23 +398,8 @@
     for j in range(1, NZ):
         dsum = dsum + dsR[mod(z + j, NZ)]
     dsum = unpack(dsum, qc)
-    pack(mgR.at[y], dsum / norm)
-    mg_y = [remote(mgR.at[y], mgR.at[y], at_y(j)) for j in YJ]
     gf = -dsum * magq / (norm * norm * norm)
     gfS[0:trials, :] = gf
-    dg = jnp.concatenate(
-        [Dq[rank * t : rank * (t + 1), :] * gf[t : t + 1] for t in range(trials)]
-        + [jnp.zeros((RP - tr, qc), F32)],
-        axis=0,
-    ).astype(BF16)
-    inner = jnp.where(same, mm(dg, Db[...], 1, 1), 0.0).astype(BF16)
-    up = SCALE * (xpT[...] + mm(dg, Wg[...], 1, 1) + SCALE * mm(inner, Ug[...], 1, 1))
-    for yy in range(NY):
-        upS[yy] = up[:tr, yy * wd : (yy + 1) * wd]
-    up_y = [remote(upS.at[mod(y + j, NY)], upR.at[y], at_y(j)) for j in YJ]
-
-    pass_twice(NZ - 4)
-    pass_twice(NZ - 3)
     for d in k_z + q_z:
         d.wait_recv()
     zrows = pl.ds(pl.multiple_of(z * 8, 8), 8)
@@ -417,22 +415,36 @@
         dnY.at[y, z],
         (SCALE * (qsum * resS[pl.ds(tz, 1), :] + ksum * gfS[pl.ds(tz, 1), :])).astype(BF16),
     )
-    dn_z = [remote(dnY.at[y, z], dnY.at[y, z], at_z(j)) for j in range(1, NZ)]
-
+    ZJ = (1, 7, 2, 6, 3, 5, 4)
+    dn_z = [remote(dnY.at[y, z], dnY.at[y, z], at_z(j)) for j in ZJ]
+    dn_y = [remote(dnY.at[y, z], dnY.at[y, z], at_y(j)) for j in YJ]
+    dg = jnp.concatenate(
+        [Dq[rank * t : rank * (t + 1), :] * gf[t : t + 1] for t in range(trials)]
+        + [jnp.zeros((RP - tr, qc), F32)],
+        axis=0,
+    ).astype(BF16)
+    inner = jnp.where(same, mm(dg, Db[...], 1, 1), 0.0).astype(BF16)
+    up = SCALE * (xpT[...] + mm(dg, Wg[...], 1, 1) + SCALE * mm(inner, Ug[...], 1, 1))
+    xpT[...] = up
+    for yy in range(NY):
+        upS[yy] = up[:tr, yy * wd : (yy + 1) * wd].astype(BF16)
+    up_y = [remote(upS.at[mod(y + j, NY)], upR.at[y], at_y(j)) for j in YJ]
+    pack(mgR.at[y], dsum / norm)
+    mg_y = [remote(mgR.at[y], mgR.at[y], at_y(j)) for j in YJ]
+    pass_twice(NZ - 3)
     pass_twice(NZ - 2)
     for d in up_y:
         d.wait_recv()
-    upP[...] = upS[y] + upR[mod(y + 1, NY)] + upR[mod(y + 2, NY)] + upR[mod(y + 3, NY)]
-    up_p = remote(upP, upPR, sib)
-
+    upP = xpT[0:tr, ywd]
+    for j in (1, 2, 3):
+        upP = upP + upR[mod(y + j, NY)].astype(F32)
+    upX[...] = upP.astype(BF16)
+    up_x = [remote(upX, upXR.at[col], dev) for dev in [at_x(j) for j in YJ] + others + [sib]]
+    for j, d in zip(ZJ, dn_z):
+        d.wait_recv()
+        piece = dnY.at[y, mod(z - j, NZ)]
+        dn_y += [remote(piece, piece, at_y(i)) for i in YJ]
     pass_twice(NZ - 1)
-    for d in dn_z:
-        d.wait_recv()
-    dn_y = [remote(dnY.at[y], dnY.at[y], at_y(j)) for j in YJ]
-
-    up_p.wait_recv()
-    upX[...] = upP[...] + upPR[...]
-    up_x = [remote(upX, upXR.at[x], at_x(j)) for j in YJ]
 
     for j in (1, 2, 3):
         x_copy(mod(x + j, NX), mod(x + j, NX)).wait_recv()
@@ -446,7 +458,9 @@
 
     for d in up_x:
         d.wait_recv()
-    out_up[...] = upX[...] + upXR[mod(x + 1, NX)] + upXR[mod(x + 2, NX)] + upXR[mod(x + 3, NX)]
+    for j in range(1, 2 * NX):
+        upP = upP + upXR[mod(col + j, 2 * NX)].astype(F32)
+    out_up[...] = upP
     for d in mg_y:
         d.wait_recv()
     out_mag[...] = mgR[...]
@@ -542,16 +556,14 @@
         V((NX, tok // 2, wd), BF16),
         V((NX, tok // 2, wd), BF16),
         V((tok // 2, wd), F32),
-        V((NY, tr, wd), F32),
-        V((NY, tr, wd), F32),
-        V((tr, wd), F32),
-        V((tr, wd), F32),
-        V((tr, wd), F32),
-        V((NX, tr, wd), F32),
+        V((NY, tr, wd), BF16),
+        V((NY, tr, wd), BF16),
+        V((tr, wd), BF16),
+        V((2 * NX, tr, wd), BF16),
         V((NY, 8, HP), F32),
         V((NY, NZ, 16, HP), BF16),
-        pltpu.SemaphoreType.DMA((112,)),
-        pltpu.SemaphoreType.DMA((112,)),
+        pltpu.SemaphoreType.DMA((144,)),
+        pltpu.SemaphoreType.DMA((144,)),
         pltpu.SemaphoreType.DMA((16,)),
         pltpu.SemaphoreType.DMA((NX,)),
         pltpu.SemaphoreType.DMA((NX,)),

time: 94.8 us -> 93.4 us (0.985); the launches traced: 93 us -> 93.2 us
  no operation moved by 1% of the time
where the time goes in v3:
time: 93.4 us; the launch traced here: 93.2 us
  Pallas kernels  92.6 us (99%)
    pallas_call x1, Pallas kernels, local(): pl.pallas_call(kernel, out_shape=(jax.ShapeDtypeStruct((tok, wd), BF16),...  90.4 us
    pallas_call x1, Pallas kernels, local(): pl.pallas_call(write_out, out_shape=(jax.ShapeDtypeStruct((tok, wd), BF16...  2.17 us

profile of v3, /device:TPU:8, one launch (start us, length us, event | category | flops | bytes accessed | tf_op | source)
XLA Modules:
  0.0 93.2 jit_solution(3339059588688923711)
XLA Ops:
  0.6 90.4 %shard_map.102 = (bf16[256,256]{1,0:T(8,128)(2,1)}, f32[4,8,512]{2,1,0:T(8,128)}, bf16[4,8,16,512]{3,2,1,0:T(8,128)(2,1)}, f32[64,256]{1,0:T(8,128)}) custom-call(bf16[256,256]{1,0:T(8,128)(2,1)} %acts.1, bf16[64,3584]{1,0:T(8,128)(2,1)} %dy.1, bf16[256,3584]{1,0:T(8,128)(2,1)} %w.1, f32[64,3584]{1,0:T(8,128)} %bitcast.8, f32[64,256]{1,0:T(8,128)} %bitcast.10, ...), custom_call_target="tpu_custom_call" | custom-call | flops 8000000000 | bytes 8000000 | tf_op jit(solution)/shard_map/pallas_call | solution.py:577
  91.1 2.2 %shard_map.103 = (bf16[256,256]{1,0:T(8,128)(2,1)}, f32[4,3584]{1,0:T(4,128)}, f32[64,3584]{1,0:T(8,128)}, f32[64,256]{1,0:T(8,128)}) custom-call(bf16[256,256]{1,0:T(8,128)(2,1)} %get-tuple-element.12.dx, f32[4,8,512]{2,1,0:T(8,128)} %get-tuple-element.13.mg, bf16[4,8,16,512]{3,2,1,0:T(8,128)(2,1)} %get-tuple-element.14.dnp, f32[64,256]{1,0:T(8,128)} %get-tuple-element.15.up), custom_call_target="tpu_custom_call" | custom-call | tf_op jit(solution)/shard_map/pallas_call | solution.py:593

commit v4 on v3

--- a/solution.py
+++ b/solution.py
@@ -8,6 +8,7 @@
 from jax.sharding import PartitionSpec as P
 
 SCALE = 2.0
+SPLIT = 96
 EPS = 1e-06
 NX, NY, NZ = 4, 4, 8
 MESH = pl.DeviceIdType.MESH
@@ -216,11 +217,11 @@
 
             @pl.when(slot != x)
             def _():
-                xs[slot] = total[:hrow].astype(BF16)
+                xs[slot] = total[:SPLIT].astype(BF16)
                 x_copy(slot, x).start()
 
             for yy in range(NY):
-                yfS[slot, yy] = total[hrow:, yy * wd : (yy + 1) * wd].astype(BF16)
+                yfS[slot, yy] = total[SPLIT:, yy * wd : (yy + 1) * wd].astype(BF16)
             for j in YJ:
                 yf_copy(slot, j).start()
 
@@ -232,7 +233,7 @@
         def _():
             for j in YJ:
                 yf_copy(slot, j).wait_recv()
-            total = dxo[slot, hrow:, ywd]
+            total = dxo[slot, SPLIT:, ywd]
             for j in (1, 2, 3):
                 total = total + yfR[slot, mod(y + j, NY)].astype(F32)
 
@@ -448,10 +449,10 @@
 
     for j in (1, 2, 3):
         x_copy(mod(x + j, NX), mod(x + j, NX)).wait_recv()
-    total = dxo[x, 0:hrow, :]
+    total = dxo[x, 0:SPLIT, :]
     for j in (1, 2, 3):
         total = total + xR[mod(x + j, NX)].astype(F32)
-    dxo[x, 0:hrow, :] = total
+    dxo[x, 0:SPLIT, :] = total
     for yy in range(NY):
         ysS[yy] = total[:, yy * wd : (yy + 1) * wd].astype(BF16)
     ys_y = [remote(ysS.at[mod(y + j, NY)], ysR.at[y], at_y(j)) for j in YJ]
@@ -466,16 +467,16 @@
     out_mag[...] = mgR[...]
     for d in ys_y:
         d.wait_recv()
-    acc = dxo[x, 0:hrow, ywd]
+    acc = dxo[x, 0:SPLIT, ywd]
     for j in (1, 2, 3):
         acc = acc + ysR[mod(y + j, NY)].astype(F32)
-    out_dx[0:hrow, :] = acc.astype(BF16)
+    out_dx[0:SPLIT, :] = acc.astype(BF16)
     for j in (1, 2, 3):
         x2_copy(mod(x + j, NX), mod(x + j, NX)).wait_recv()
     acc = acc1[...]
     for j in (1, 2, 3):
         acc = acc + x2R[mod(x + j, NX)].astype(F32)
-    out_dx[hrow:, :] = acc.astype(BF16)
+    out_dx[SPLIT:, :] = acc.astype(BF16)
 
     for d in dn_y:
         d.wait_recv()
@@ -547,15 +548,15 @@
         V((NX, tok, width), F32),
         V((NX, tok, width), BF16),
         V((NX, tok, width), BF16),
-        V((NX, tok // 2, width), BF16),
-        V((NX, tok // 2, width), BF16),
-        V((NY, tok // 2, wd), BF16),
-        V((NY, tok // 2, wd), BF16),
-        V((NX, NY, tok // 2, wd), BF16),
-        V((NX, NY, tok // 2, wd), BF16),
-        V((NX, tok // 2, wd), BF16),
-        V((NX, tok // 2, wd), BF16),
-        V((tok // 2, wd), F32),
+        V((NX, SPLIT, width), BF16),
+        V((NX, SPLIT, width), BF16),
+        V((NY, SPLIT, wd), BF16),
+        V((NY, SPLIT, wd), BF16),
+        V((NX, NY, tok - SPLIT, wd), BF16),
+        V((NX, NY, tok - SPLIT, wd), BF16),
+        V((NX, tok - SPLIT, wd), BF16),
+        V((NX, tok - SPLIT, wd), BF16),
+        V((tok - SPLIT, wd), F32),
         V((NY, tr, wd), BF16),
         V((NY, tr, wd), BF16),
         V((tr, wd), BF16),

time: 93.4 us -> 93 us (level)
  Pallas kernels: 92.6 us -> 91.6 us
    pallas_call x1, Pallas kernels: 90.4 us -> 89.4 us  [local(): pl.pallas_call(kernel, out_shape=(jax.ShapeDtypeStruct((tok, wd), BF16),...]
where the time goes in v4:
time: 93 us; the launch traced here: 92.2 us
  Pallas kernels  91.6 us (98%)
    pallas_call x1, Pallas kernels, local(): pl.pallas_call(kernel, out_shape=(jax.ShapeDtypeStruct((tok, wd), BF16),...  89.4 us
    pallas_call x1, Pallas kernels, local(): pl.pallas_call(write_out, out_shape=(jax.ShapeDtypeStruct((tok, wd), BF16...  2.17 us

profile of v4, /device:TPU:8, one launch (start us, length us, event | category | flops | bytes accessed | tf_op | source)
XLA Modules:
  0.0 92.2 jit_solution(5148186875766050935)
XLA Ops:
  0.6 89.4 %shard_map.102 = (bf16[256,256]{1,0:T(8,128)(2,1)}, f32[4,8,512]{2,1,0:T(8,128)}, bf16[4,8,16,512]{3,2,1,0:T(8,128)(2,1)}, f32[64,256]{1,0:T(8,128)}) custom-call(bf16[256,256]{1,0:T(8,128)(2,1)} %acts.1, bf16[64,3584]{1,0:T(8,128)(2,1)} %dy.1, bf16[256,3584]{1,0:T(8,128)(2,1)} %w.1, f32[64,3584]{1,0:T(8,128)} %bitcast.8, f32[64,256]{1,0:T(8,128)} %bitcast.10, ...), custom_call_target="tpu_custom_call" | custom-call | flops 8000000000 | bytes 8000000 | tf_op jit(solution)/shard_map/pallas_call | solution.py:578
  90.0 2.2 %shard_map.103 = (bf16[256,256]{1,0:T(8,128)(2,1)}, f32[4,3584]{1,0:T(4,128)}, f32[64,3584]{1,0:T(8,128)}, f32[64,256]{1,0:T(8,128)}) custom-call(bf16[256,256]{1,0:T(8,128)(2,1)} %get-tuple-element.12.dx, f32[4,8,512]{2,1,0:T(8,128)} %get-tuple-element.13.mg, bf16[4,8,16,512]{3,2,1,0:T(8,128)(2,1)} %get-tuple-element.14.dnp, f32[64,256]{1,0:T(8,128)} %get-tuple-element.15.up), custom_call_target="tpu_custom_call" | custom-call | tf_op jit(solution)/shard_map/pallas_call | solution.py:594
